TPU v7x, 256 devices: a whole 4x4x8 slice. The times are simulated.
256 devices in a mesh: expert: 32 (over x_hi, z, core), blk: 8 (over x_lo, y).
Axes of the slice: x: 4 (x_hi: 2, x_lo: 2; x = x_hi * 2 + x_lo), y: 4, z: 8, core: 2. Of those that a mesh axis runs over, the one named last changes fastest.
Arguments:
- tokens: bfloat16 [8192, 7168], P('expert', 'blk'), may hold values from -6 to 6
- cotangent: bfloat16 [8192, 7168], P('expert', 'blk'), may hold values from -6 to 6
- expert_ids: int32 [8192, 8], P('expert'), may hold values from 0 to 255, as said below
- gate_fixed: int32 [8192, 8], P('expert'), may hold values from 4096 to 65535
- w_gate: bfloat16 [32, 7168, 1024], P('expert', 'blk'), may hold values from -0.0625 to 0.0625
- w_up: bfloat16 [32, 7168, 1024], P('expert', 'blk'), may hold values from -0.0625 to 0.0625
- w_down: bfloat16 [32, 1024, 7168], P('expert', None, 'blk'), may hold values from -0.1875 to 0.1875
Outputs:
- layer_out: bfloat16 [8192, 7168], P('expert', 'blk')
- grad_gate: bfloat16 [32, 7168, 1024], P('expert', 'blk')
- grad_up: bfloat16 [32, 7168, 1024], P('expert', 'blk')
- grad_down: bfloat16 [32, 1024, 7168], P('expert', None, 'blk')
- loads: int32 [256], replicated
Inputs may be any that keep to these rules, and one draw needn't show every extreme that they name: `expert_ids`: each token names 8 different experts. Among the tokens of one index of expert no expert is named by more than 16 tokens, and some expert below 32 is named by exactly 16 tokens of every index.
All inputs are finite; a program needn't handle non-finite values.
Results may differ from a plain program's by a relative error of at most 0.029.
Values may be sent and summed in bfloat16 or wider, within the bound.
No kernel may reach another device: no remote copies, remote signals or barrier semaphores. Data moves between devices by JAX's collectives and lax.ppermute only.
A program may use at most 64 MiB of HBM per device.

v0:
```python
import jax
import jax.numpy as jnp
from jax import lax
from jax.sharding import PartitionSpec as P

EXPERTS_ALL = 256
TOPK = 8
CAP = 16


def matmul(left, right):
    return jnp.dot(left, right, preferred_element_type=jnp.float32)


def contract_rows(left, right):
    return lax.dot_general(
        left, right, (((0,), (0,)), ((), ())), preferred_element_type=jnp.float32
    )


def count_picks(picked_ids):
    flat_ids = picked_ids.reshape(-1)
    table = jnp.arange(EXPERTS_ALL, dtype=jnp.int32)
    return jnp.sum((flat_ids[:, None] == table[None, :]).astype(jnp.int32), axis=0)


def body(tokens, cotangent, expert_ids, gate_fixed, w_gate, w_up, w_down):
    experts = lax.axis_size("expert")
    tok_rows = tokens.shape[0]
    feature_cols = tokens.shape[1]
    total_slots = experts * CAP
    gate_values = gate_fixed.astype(jnp.float32) * (1.0 / 65536.0)
    picked_ids = expert_ids.reshape(-1)
    inside = picked_ids < experts
    onehot = (picked_ids[:, None] == jnp.arange(experts, dtype=jnp.int32)[None, :]).astype(
        jnp.int32
    )
    rank_in = jnp.sum((jnp.cumsum(onehot, axis=0) - onehot) * onehot, axis=1)
    slot_of = jnp.where(inside, picked_ids * CAP + rank_in, total_slots).reshape(tok_rows, TOPK)
    matches = (
        jnp.arange(total_slots, dtype=jnp.int32)[:, None, None] == slot_of[None, :, :]
    ).astype(jnp.float32)
    select = jnp.sum(matches, axis=2)
    slot_gate = jnp.sum(matches * gate_values[None, :, :], axis=(1, 2))
    select_bf = select.astype(jnp.bfloat16)
    routed_x = matmul(select_bf, tokens).astype(jnp.bfloat16).reshape(experts, CAP, feature_cols)
    routed_cot = (slot_gate[:, None] * matmul(select_bf, cotangent)).astype(jnp.bfloat16)
    routed_cot = routed_cot.reshape(experts, CAP, feature_cols)
    arrived_x, arrived_cot = (
        lax.all_to_all(routed_x, "expert", split_axis=0, concat_axis=0, tiled=True),
        lax.all_to_all(routed_cot, "expert", split_axis=0, concat_axis=0, tiled=True),
    )
    arrived = arrived_x.reshape(-1, feature_cols)
    gate_slab = w_gate[0]
    up_slab = w_up[0]
    down_slab = w_down[0]
    projected = jnp.stack([matmul(arrived, gate_slab), matmul(arrived, up_slab)], axis=1)
    projected = lax.psum(projected.astype(jnp.bfloat16), "blk").astype(jnp.float32)
    gate_pre = projected[:, 0]
    up_pre = projected[:, 1]
    sigma = jax.nn.sigmoid(gate_pre)
    hidden = (gate_pre * sigma * up_pre).astype(jnp.bfloat16)
    expert_out = matmul(hidden, down_slab).astype(jnp.bfloat16).reshape(experts, CAP, feature_cols)
    returned = lax.all_to_all(expert_out, "expert", split_axis=0, concat_axis=0, tiled=True)
    padded_rows = jnp.concatenate(
        [returned.reshape(total_slots, feature_cols), jnp.zeros((1, feature_cols), jnp.bfloat16)],
        axis=0,
    )
    pick_rows = padded_rows[slot_of]
    layer_out = jnp.sum(gate_values[:, :, None] * pick_rows.astype(jnp.float32), axis=1).astype(
        jnp.bfloat16
    )
    arrived_grad = arrived_cot.reshape(-1, feature_cols)
    partial_back = lax.dot_general(
        arrived_grad, down_slab, (((1,), (1,)), ((), ())), preferred_element_type=jnp.float32
    )
    d_hidden = lax.psum(partial_back.astype(jnp.bfloat16), "blk").astype(jnp.float32)
    d_gate = (d_hidden * up_pre * sigma * (1.0 + gate_pre * (1.0 - sigma))).astype(jnp.bfloat16)
    d_up = (d_hidden * gate_pre * sigma).astype(jnp.bfloat16)
    grad_down = contract_rows(hidden, arrived_grad).astype(jnp.bfloat16)[None]
    grad_gate = contract_rows(arrived, d_gate).astype(jnp.bfloat16)[None]
    grad_up = contract_rows(arrived, d_up).astype(jnp.bfloat16)[None]
    loads = lax.psum(count_picks(expert_ids), "expert")
    return (layer_out, grad_gate, grad_up, grad_down, loads)


def solution(mesh):
    return jax.shard_map(
        body,
        mesh=mesh,
        in_specs=(
            P("expert", "blk"),
            P("expert", "blk"),
            P("expert", None),
            P("expert", None),
            P("expert", "blk", None),
            P("expert", "blk", None),
            P("expert", None, "blk"),
        ),
        out_specs=(
            P("expert", "blk"),
            P("expert", "blk", None),
            P("expert", "blk", None),
            P("expert", None, "blk"),
            P(),
        ),
        check_vma=False,
    )
```

profile of v0, /device:TPU:1, one launch (start us, length us, event | category | flops | bytes accessed | tf_op | source)
XLA Modules:
  0.0 269.7 jit_solution(6837780962086399437)
XLA Ops:
  8.4 9.1 %reduce-window.6 = s32[32,16,128]{2,1,0:T(8,128)S(1)} reduce-window(s32[32,16,128]{2,1,0:T(8,128)S(1)} %fusion.43, s32[]{:T(128)} %constant.5.clone.1), window={size=1x1x128 pad=0_0x0_0x127_0}, to_apply=%region_0.0 | reduce-window | flops 8323072 | bytes 524292 | tf_op jit(solution)/shard_map/reduce-window
  18.6 2.1 select_reduce_fusion
  20.7 1.4 convolution_convert_fusion
  22.0 12.6 %all-to-all-start = ((bf16[32,16,896]{2,1,0:T(8,128)(2,1)}), bf16[32,16,896]{2,1,0:T(8,128)(2,1)S(1)}, u32[]{:S(2)}, u32[]{:S(2)}) async-start(bf16[32,16,896]{2,1,0:T(8,128)(2,1)} %bitcast.3), calls=%async_computation | async-start | bytes 1835008 | tf_op jit(solution)/shard_map/all_to_all | solution.py:50
  34.6 1.4 multiply_convert_fusion.1
  36.0 23.7 %all-to-all-done = bf16[32,16,896]{2,1,0:T(8,128)(2,1)S(1)} async-done(((bf16[32,16,896]{2,1,0:T(8,128)(2,1)}), bf16[32,16,896]{2,1,0:T(8,128)(2,1)S(1)}, u32[]{:S(2)}, u32[]{:S(2)}) %all-to-all-start) | async-done | bytes 917536 | tf_op jit(solution)/shard_map/all_to_all | solution.py:50
  59.7 6.8 %all-to-all-start.2 = ((bf16[32,16,896]{2,1,0:T(8,128)(2,1)}), bf16[32,16,896]{2,1,0:T(8,128)(2,1)}, u32[]{:S(2)}, u32[]{:S(2)}) async-start(bf16[32,16,896]{2,1,0:T(8,128)(2,1)} %bitcast.14), calls=%async_computation.2 | async-start | bytes 1835008 | tf_op jit(solution)/shard_map/all_to_all | solution.py:51
  66.6 2.9 %fusion.30 = bf16[512,1,1024]{2,0,1:T(8,128)(2,1)S(1)} fusion(bf16[512,896]{1,0:T(8,128)(2,1)S(1)} %bitcast.102, bf16[1,896,1024]{2,1,0:T(8,128)(2,1)} %param.12), kind=kOutput, calls=%fused_computation.40 | convolution fusion | flops 940048384 | bytes 3801088 | tf_op jit(solution)/shard_map/dot_general | solution.py:12
  69.5 1.3 fusion.33
  70.8 1.5 pad_maximum_fusion
  72.2 19.5 %all-to-all-done.2 = bf16[32,16,896]{2,1,0:T(8,128)(2,1)} async-done(((bf16[32,16,896]{2,1,0:T(8,128)(2,1)}), bf16[32,16,896]{2,1,0:T(8,128)(2,1)}, u32[]{:S(2)}, u32[]{:S(2)}) %all-to-all-start.2) | async-done | bytes 917536 | tf_op jit(solution)/shard_map/all_to_all | solution.py:51
  91.8 3.4 %fusion.24 = bf16[512,1024]{1,0:T(8,128)(2,1)} fusion(bf16[512,896]{1,0:T(8,128)(2,1)} %bitcast.15, bf16[1,1024,896]{2,1,0:T(8,128)(2,1)S(1)} %copy-done), kind=kOutput, calls=%fused_computation.37 | convolution fusion | flops 940048384 | bytes 3801088 | tf_op jit(solution)/shard_map/dot_general | solution.py:74
  95.2 91.5 %all-reduce.4.cloned.1.call-done = (bf16[512,2,1024]{2,0,1:T(8,128)(2,1)}, bf16[512,1024]{1,0:T(8,128)(2,1)}) async-done(((bf16[512,2,1024]{2,0,1:T(8,128)(2,1)}, bf16[512,1024]{1,0:T(8,128)(2,1)}), (bf16[512,2,1024]{2,0,1:T(8,128)(2,1)}, bf16[512,1024]{1,0:T(8,128)(2,1)})) %all-reduce.4.cloned.1.call-update) | async-done | bytes 3145744 | tf_op jit(solution)/shard_map/psum | solution.py:58
  186.8 2.0 convert_element_type.72
  189.4 1.3 copy-done.1
  190.7 2.2 fusion.27
  192.9 11.7 %all-to-all-start.1 = ((bf16[32,16,896]{2,1,0:T(8,128)(2,1)}), bf16[32,16,896]{2,1,0:T(8,128)(2,1)S(1)}, u32[]{:S(2)}, u32[]{:S(2)}) async-start(bf16[32,16,896]{2,1,0:T(8,128)(2,1)} %bitcast.106), calls=%async_computation.1 | async-start | bytes 1835008 | tf_op jit(solution)/shard_map/all_to_all | solution.py:64
  205.4 31.4 %psum.23 = s32[256]{0:T(256)} all-reduce(s32[256]{0:T(256)S(1)} %convert_reduce_fusion.1), channel_id=1, replica_groups=mesh['expert'=32,'blk'=8] {'expert'}, use_global_device_ids=true, to_apply=%region_9.10 | all-reduce | flops 256 | bytes 2048 | tf_op jit(solution)/shard_map/psum | solution.py:83
  236.8 4.2 %convert_bitcast_fusion = bf16[1,1024,896]{2,1,0:T(8,128)(2,1)} fusion(bf16[512,896]{1,0:T(8,128)(2,1)} %bitcast.15, bf16[512,1,1024]{2,0,1:T(8,128)(2,1)} %copy-done.4), kind=kOutput, calls=%fused_computation.31 | convolution fusion | flops 940441600 | bytes 3801088 | tf_op jit(solution)/shard_map/dot_general | solution.py:16
  241.0 2.5 convert_bitcast_fusion.1
  243.4 2.5 convert_bitcast_fusion.2
  246.9 1.3 concatenate.3
  248.2 9.5 %gather_fusion = bf16[2048,896]{1,0:T(8,128)(2,1)} fusion(bf16[513,896]{1,0:T(8,128)(2,1)S(1)} %concatenate.3, s32[2048]{0:T(1024)S(1)} %broadcast_clamp_fusion), kind=kCustom, calls=%fused_computation | custom fusion | bytes 7348224 | tf_op jit(solution)/shard_map/gather | solution.py:69
  257.7 5.1 %fusion = bf16[256,896]{1,0:T(8,128)(2,1)} fusion(bf16[2048,896]{1,0:T(8,128)(2,1)} %gather_fusion, f32[256,8]{1,0:T(8,128)S(1)} %copy.35), kind=kLoop, calls=%fused_computation.2 | loop fusion | flops 5275648 | bytes 4136960 | tf_op jit(solution)/shard_map/reduce_sum | solution.py:70
  (47 shorter events, 4.6 us)
Async XLA Ops:
  7.2 84.6 %copy-start = (bf16[1,1024,896]{2,1,0:T(8,128)(2,1)S(1)}, bf16[1,1024,896]{2,1,0:T(8,128)(2,1)}, u32[]{:S(2)}) copy-start(bf16[1,1024,896]{2,1,0:T(8,128)(2,1)} %param.13) | copy-start | bytes 5505028
  7.2 11.3 %copy-start.9 = (s32[256,8]{0,1:T(8,128)S(1)}, s32[256,8]{0,1:T(8,128)}, u32[]{:S(2)}) copy-start(s32[256,8]{0,1:T(8,128)} %param.9) | copy-start | bytes 24580
  7.2 11.4 %copy-start.10 = (s32[256,8]{0,1:T(8,128)S(1)}, s32[256,8]{0,1:T(8,128)}, u32[]{:S(2)}) copy-start(s32[256,8]{0,1:T(8,128)} %param.10) | copy-start | bytes 24580
  7.2 13.4 %copy-start.7 = (bf16[256,896]{1,0:T(8,128)(2,1)S(1)}, bf16[256,896]{1,0:T(8,128)(2,1)}, u32[]{:S(2)}) copy-start(bf16[256,896]{1,0:T(8,128)(2,1)} %param.7) | copy-start | bytes 1376260
  18.3 16.3 %copy-start.8 = (bf16[256,896]{1,0:T(8,128)(2,1)S(1)}, bf16[256,896]{1,0:T(8,128)(2,1)}, u32[]{:S(2)}) copy-start(bf16[256,896]{1,0:T(8,128)(2,1)} %param.8) | copy-start | bytes 1376260
  22.0 37.6 %all-to-all-start = ((bf16[32,16,896]{2,1,0:T(8,128)(2,1)}), bf16[32,16,896]{2,1,0:T(8,128)(2,1)S(1)}, u32[]{:S(2)}, u32[]{:S(2)}) async-start(bf16[32,16,896]{2,1,0:T(8,128)(2,1)} %bitcast.3), calls=%async_computation | async-start | bytes 1835008 | tf_op jit(solution)/shard_map/all_to_all | solution.py:50
  59.7 9.8 %copy-start.5 = (bf16[32,16,896]{2,1,0:T(8,128)(2,1)}, bf16[32,16,896]{2,1,0:T(8,128)(2,1)S(1)}, u32[]{:S(2)}) copy-start(bf16[32,16,896]{2,1,0:T(8,128)(2,1)S(1)} %all-to-all-done) | copy-start | bytes 2752516
  59.7 32.1 %all-to-all-start.2 = ((bf16[32,16,896]{2,1,0:T(8,128)(2,1)}), bf16[32,16,896]{2,1,0:T(8,128)(2,1)}, u32[]{:S(2)}, u32[]{:S(2)}) async-start(bf16[32,16,896]{2,1,0:T(8,128)(2,1)} %bitcast.14), calls=%async_computation.2 | async-start | bytes 1835008 | tf_op jit(solution)/shard_map/all_to_all | solution.py:51
  66.5 120.3 %all-reduce.4.cloned.1.call-start = ((), (), s32[]{:S(2)}) async-start(), calls=%async_computation.3 | async-start | bytes 6291456 | tf_op jit(solution)/shard_map/psum | solution.py:58
  66.5 2.9 %copy-start.11 = (bf16[1,896,1024]{2,1,0:T(8,128)(2,1)S(1)}, bf16[1,896,1024]{2,1,0:T(8,128)(2,1)}, u32[]{:S(2)}) copy-start(bf16[1,896,1024]{2,1,0:T(8,128)(2,1)} %param.11) | copy-start | bytes 5505028
  188.8 1.9 copy-start.1
  190.7 2.2 copy-start.4
  192.9 53.1 %all-to-all-start.1 = ((bf16[32,16,896]{2,1,0:T(8,128)(2,1)}), bf16[32,16,896]{2,1,0:T(8,128)(2,1)S(1)}, u32[]{:S(2)}, u32[]{:S(2)}) async-start(bf16[32,16,896]{2,1,0:T(8,128)(2,1)} %bitcast.106), calls=%async_computation.1 | async-start | bytes 1835008 | tf_op jit(solution)/shard_map/all_to_all | solution.py:64
  236.8 4.2 %copy-start.2 = (f32[512,2,1024]{2,0,1:T(8,128)S(1)}, f32[512,2,1024]{2,0,1:T(8,128)}, u32[]{:S(2)}) copy-start(f32[512,2,1024]{2,0,1:T(8,128)} %copy-done.1) | copy-start | bytes 12582916
  236.8 4.2 %copy-start.6 = (bf16[32,16,896]{2,1,0:T(8,128)(2,1)S(1)}, bf16[32,16,896]{2,1,0:T(8,128)(2,1)}, u32[]{:S(2)}) copy-start(bf16[32,16,896]{2,1,0:T(8,128)(2,1)} %copy-done.5) | copy-start | bytes 2752516
  236.8 4.2 %copy-start.12 = (bf16[512,1024]{1,0:T(8,128)(2,1)S(1)}, bf16[512,1024]{1,0:T(8,128)(2,1)}, u32[]{:S(2)}) copy-start(bf16[512,1024]{1,0:T(8,128)(2,1)} %get-tuple-element.8) | copy-start | bytes 3145732
  246.0 0.9 copy-start.3
Sparse Core Ops, SparseCore 0:
  95.3 91.3 all-reduce.3
where the time goes:
time: 272 us; the launch traced here: 270 us
  waiting for transfers between devices  135 us (50%)
  blocking collectives  31.4 us (12%)
  starting transfers between devices  31.2 us (11%)
  matrix products  21.7 us (8%)
  other arithmetic  21.2 us (8%)
  local copies, waits for them, and re-layouts  15.1 us (6%)
  between operations  14.3 us (5%)
    psum x1, waiting for transfers between devices, body(): lax.psum(projected.astype(jnp.bfloat16), 'blk').astype(jnp.float32)  91.5 us
    psum x1, blocking collectives, body(): loads = lax.psum(count_picks(expert_ids), 'expert')  31.4 us
    all_to_all x1, waiting for transfers between devices, body(): lax.all_to_all(routed_x, 'expert', split_axis=0, concat_axis=0, tiled=True)  23.7 us
    all_to_all x1, waiting for transfers between devices, body(): lax.all_to_all(routed_cot, 'expert', split_axis=0, concat_axis=0, tiled=T...  19.5 us
    all_to_all x1, starting transfers between devices, body(): lax.all_to_all(routed_x, 'expert', split_axis=0, concat_axis=0, tiled=True)  12.6 us
    all_to_all x1, starting transfers between devices, body(): lax.all_to_all(expert_out, 'expert', split_axis=0, concat_axis=0, tiled=T...  11.7 us
    gather x1, local copies, waits for them, and re-layouts, body(): pick_rows = padded_rows[slot_of]  9.52 us
    another operation x3, other arithmetic  9.41 us
  transfers between devices with their start and end apart: 4, of which 3 were waited for; matrix products, arithmetic and copies ran while one was open for 6% of the time, Pallas kernels for 0%

commit v1 on v0

v1 whole, which is shorter than its diff:
```python
import jax
import jax.numpy as jnp
from jax import lax
from jax.experimental import pallas as pl
from jax.experimental.pallas import tpu as pltpu
from jax.sharding import PartitionSpec as P

EXPERTS_ALL = 256
TOPK = 8
CAP = 16
N_Y = 4
TILE = 256
F32 = jnp.float32
BF16 = jnp.bfloat16
MIB = 1024 * 1024
SMALL = 16 * MIB
LARGE = 58 * MIB
COUNT_LANES = 128


def iota(shape, dim):
    return lax.broadcasted_iota(jnp.int32, shape, dim)


def dot(left, right, dims):
    return lax.dot_general(left, right, (dims, ((), ())), preferred_element_type=F32)


def matmul(left, right):
    return jnp.dot(left, right, preferred_element_type=F32)


def rows_of(order_ref, d, chunk):
    return pl.ds(pl.multiple_of(order_ref[d] * chunk, chunk), chunk)


def columns_of(i):
    return pl.ds(pl.multiple_of(i * TILE, TILE), TILE)


def whole(array):
    zeros = (0,) * len(array.shape)
    return pl.BlockSpec(array.shape, lambda i: zeros)


def call(kernel, outs, *args, ordered=False, stay=(), limit=SMALL, flops=0, traffic=0, **options):
    outs = [jax.ShapeDtypeStruct(s, t) for s, t in outs]
    in_specs = [whole(a) for a in args]
    if ordered:
        in_specs[0] = pl.BlockSpec(memory_space=pltpu.SMEM)
    for i in stay:
        in_specs[i] = pl.BlockSpec(memory_space=pltpu.HBM)
    settings = dict(grid=(1,), in_specs=in_specs, out_specs=[whole(o) for o in outs])
    settings.update(options)
    return pl.pallas_call(
        kernel,
        out_shape=outs,
        compiler_params=pltpu.CompilerParams(vmem_limit_bytes=limit),
        cost_estimate=pl.CostEstimate(flops=flops, bytes_accessed=traffic, transcendentals=0),
        name=kernel.__name__,
        **settings,
    )(*args)


def ones_where(condition):
    return condition.astype(F32).astype(BF16)


def spread_of(slots, experts):
    return ones_where((iota((slots, experts), 0) // CAP) == iota((slots, experts), 1))


def slots_of(ids_ref, slots):
    rows = ids_ref.shape[1]
    experts = slots // CAP
    line = iota((experts, rows), 0)
    picked = jnp.zeros((experts, rows), F32)
    for k in range(TOPK):
        picked = jnp.where(ids_ref[k : k + 1, :] == line, 1.0, picked)
    rank = matmul(picked.astype(BF16), ones_where(iota((rows, rows), 0) < iota((rows, rows), 1)))
    key = jnp.where(picked > 0.5, rank, -1.0).astype(BF16)
    slot_rank = (iota((slots, rows), 0) % CAP).astype(F32)
    return (matmul(spread_of(slots, experts), key) == slot_rank).astype(F32)


def route(ids_ref, tok_ref, rx_ref):
    sel = slots_of(ids_ref, rx_ref.shape[0]).astype(BF16)
    rx_ref[...] = matmul(sel, tok_ref[...]).astype(BF16)


def route_back(ids_ref, gate_ref, cot_ref, rc_ref, gate_hi_ref, gate_lo_ref):
    rows, cols = cot_ref.shape
    slots = rc_ref.shape[0]
    experts = slots // CAP
    line = iota((experts, rows), 0)
    gate = jnp.zeros((experts, rows), jnp.int32)
    for k in range(TOPK):
        gate = jnp.where(ids_ref[k : k + 1, :] == line, gate_ref[k : k + 1, :], gate)
    spread = spread_of(slots, experts)
    select = slots_of(ids_ref, slots)
    hi = matmul(spread, (gate // 256).astype(F32).astype(BF16)) * select
    lo = matmul(spread, (gate % 256).astype(F32).astype(BF16)) * select
    slot_gate = jnp.sum(hi * 256.0 + lo, axis=1, keepdims=True) * (1.0 / 65536.0)
    rc_ref[:, :cols] = (slot_gate * matmul(select.astype(BF16), cot_ref[...])).astype(BF16)
    gate_hi_ref[...] = hi.T.astype(BF16)
    gate_lo_ref[...] = lo.T.astype(BF16)
    every = iota((EXPERTS_ALL, rows), 0)
    hits = jnp.zeros((EXPERTS_ALL, rows), F32)
    for k in range(TOPK):
        hits = hits + jnp.where(ids_ref[k : k + 1, :] == every, 1.0, 0.0)
    counts = dot(jnp.ones((CAP, rows), BF16), hits.astype(BF16), ((1,), (1,)))
    line = iota((CAP, COUNT_LANES), 0)
    block = jnp.where(line == 0, counts[:, :COUNT_LANES], jnp.where(line == 1, counts[:, COUNT_LANES:], 0.0))
    block = block.astype(BF16)
    for e in range(experts):
        rc_ref[e * CAP : (e + 1) * CAP, cols:] = block


def turn(order_ref, x_ref, out_ref, held):
    chunk = x_ref.shape[0] // order_ref.shape[0]
    for d in range(order_ref.shape[0]):
        held[d * chunk : (d + 1) * chunk, :] = x_ref[rows_of(order_ref, d, chunk), :]
    out_ref[...] = held[...].T


def in_order(order_ref, x_ref, held):
    @pl.when(pl.program_id(0) == 0)
    def _():
        n = order_ref.shape[0]
        chunk = x_ref.shape[0] // n
        for d in range(n):
            held[d * chunk : (d + 1) * chunk, :] = x_ref[rows_of(order_ref, d, chunk), : held.shape[1]]


def project(order_ref, x_ref, wg_ref, wu_ref, far_ref, near_ref, *rest):
    ups, held = rest[:-1], rest[-1]
    chunk = far_ref.shape[1]
    in_order(order_ref, x_ref, held)
    gate = matmul(held[...], wg_ref[...]).astype(BF16)
    up = matmul(held[...], wu_ref[...]).astype(BF16)
    for dx in range(2):
        for dy in range(N_Y):
            at = (dx * N_Y + dy) * chunk
            (near_ref, far_ref)[dx][dy] = gate[at : at + chunk]
            ups[dy][dx] = up[at : at + chunk]


def meet_near(near_ref, got_ref, *outs):
    for dy, out in enumerate(outs, 1):
        out[...] = (near_ref[dy].astype(F32) + got_ref[dy].astype(F32)).astype(BF16)


def meet_far(*refs):
    out = refs[-1]
    out[...] = sum(r[1].astype(F32) for r in refs[:-1]).astype(BF16)


def activate(near_ref, got_ref, g1, g2, g3, u0, u1, u2, u3, got_u, part_ref, *rest):
    outs, (gate_ref, up_ref) = rest[:-2], rest[-2:]
    gate = near_ref[0].astype(F32) + got_ref[0].astype(F32)
    for r in (g1, g2, g3):
        gate = gate + r[...].astype(F32)
    up = got_u[...].astype(F32)
    for r in (u0, u1, u2, u3):
        up = up + r[0].astype(F32)
    gate_ref[...] = gate
    up_ref[...] = up
    hidden = (gate * jax.nn.sigmoid(gate) * up).astype(BF16)
    for d, out in enumerate(outs):
        out[0] = hidden
        out[1] = part_ref[d]


def back(order_ref, c_ref, w_ref, part_ref, load_ref, held):
    slots, cols = held.shape
    chunk = part_ref.shape[1]
    in_order(order_ref, c_ref, held)
    partial = dot(held[...], w_ref[...], ((1,), (1,))).astype(BF16)
    for d in range(part_ref.shape[0]):
        part_ref[d] = partial[d * chunk : (d + 1) * chunk]

    @pl.when(pl.program_id(0) == 0)
    def _():
        counted = ones_where(iota((8, slots), 1) % CAP == iota((8, slots), 0))
        load_ref[...] = matmul(counted, c_ref[:, cols:]).astype(jnp.int32)


def expert(order_ref, w_ref, *rest):
    pieces, (out_ref, hidden_ref) = rest[:-2], rest[-2:]
    chunk = pieces[0].shape[1]
    for d, piece in enumerate(pieces):
        hidden_ref[rows_of(order_ref, d, chunk), :] = piece[0]
    out_ref[...] = matmul(hidden_ref[...], w_ref[...]).astype(BF16)


def back_act(gate_ref, up_ref, *rest):
    parts, (dg_ref, du_ref) = rest[:-2], rest[-2:]
    d = sum(r[1].astype(F32) for r in parts)
    gate = gate_ref[...]
    sigma = jax.nn.sigmoid(gate)
    dg_ref[...] = (d * up_ref[...] * sigma * (1.0 + gate * (1.0 - sigma))).astype(BF16)
    du_ref[...] = (d * gate * sigma).astype(BF16)


def grad_down_tile(hidden_ref, c_ref, out_ref):
    out_ref[...] = matmul(hidden_ref[...].T, c_ref[:, : out_ref.shape[1]]).astype(BF16)


def grad_tile(x_ref, g0, g1, g2, g3, u0, u1, out_g, out_u, held_g, held_u):
    chunk = g0.shape[1]
    for dx in range(2):
        for dy in range(N_Y):
            at = (dx * N_Y + dy) * chunk
            held_g[at : at + chunk, :] = (g0, g1, g2, g3)[dy][dx]
            held_u[at : at + chunk, :] = (u0, u1)[dx][dy]
    x = x_ref[...]
    out_g[...] = matmul(x, held_g[...]).astype(BF16)
    out_u[...] = matmul(x, held_u[...]).astype(BF16)


def combine(hi_ref, lo_ref, y_ref, out_ref):
    y = y_ref[...]
    out = matmul(hi_ref[...], y) * (1.0 / 256.0) + matmul(lo_ref[...], y) * (1.0 / 65536.0)
    out_ref[...] = out.astype(BF16)


def block_at(d):
    me = lax.axis_index("blk")
    return lax.rem(me // N_Y + d // N_Y, 2) * N_Y + lax.rem(me % N_Y + d % N_Y, N_Y)


def move(array, d):
    n = lax.axis_size("blk")
    pairs = [(i, (i // N_Y + d // N_Y) % 2 * N_Y + (i + d) % N_Y) for i in range(n)]
    return lax.ppermute(array, "blk", pairs)


def to_experts(rows, experts):
    cols = rows.shape[-1]
    out = lax.all_to_all(rows.reshape(experts, CAP, cols), "expert", split_axis=0, concat_axis=0, tiled=True)
    return out.reshape(-1, cols)


def body(tokens, cotangent, expert_ids, gate_fixed, w_gate, w_up, w_down):
    experts = lax.axis_size("expert")
    n_blk = lax.axis_size("blk")
    rows, cols = tokens.shape
    ff = w_gate.shape[2]
    slots = experts * CAP
    chunk = slots // n_blk
    steps = ff // TILE
    goes_to = jnp.stack([block_at(d) for d in range(n_blk)])
    comes_from = jnp.stack([block_at((d // N_Y) * N_Y + (-d) % N_Y) for d in range(n_blk)])
    ids = expert_ids.T
    part = (chunk, ff)

    order = (4, 1, 3, 2, 5, 6, 7)

    def tiles(*block):
        zeros = (0,) * (len(block) - 1)
        return pl.BlockSpec(block, lambda i: zeros + (i,))

    def fixed(*block):
        zeros = (0,) * len(block)
        return pl.BlockSpec(block, lambda i: zeros)

    table = pl.BlockSpec(memory_space=pltpu.SMEM)
    (routed_x,) = call(route, [((slots, cols), BF16)], ids, tokens, limit=LARGE)
    arrived = to_experts(routed_x, experts)
    routed_cot, gate_hi, gate_lo = call(
        route_back,
        [((slots, cols + COUNT_LANES), BF16), ((rows, slots), BF16), ((rows, slots), BF16)],
        ids,
        gate_fixed.T,
        cotangent,
        limit=LARGE,
    )
    routed_cot, goes_to, comes_from = lax.optimization_barrier((routed_cot, goes_to, comes_from))
    shapes = [(N_Y, chunk)] * 2 + [(2, chunk)] * N_Y
    far, near, *ups = call(
        project,
        [(a + (ff,), BF16) for a in shapes],
        goes_to,
        arrived,
        w_gate[0],
        w_up[0],
        grid=(steps,),
        in_specs=[table, fixed(slots, cols), tiles(cols, TILE), tiles(cols, TILE)],
        out_specs=[tiles(*a, TILE) for a in shapes],
        scratch_shapes=[pltpu.VMEM((slots, cols), BF16)],
        limit=LARGE,
        flops=4 * slots * cols * ff,
        traffic=7_000_000,
    )
    arrived_cot = to_experts(routed_cot, experts)

    got_far = move(far, N_Y)
    got_ups = [ups[0]] + [move(ups[dy], dy) for dy in range(1, N_Y)]
    (turned,) = call(
        turn,
        [((cols, slots), BF16)],
        comes_from,
        arrived,
        ordered=True,
        scratch_shapes=[pltpu.VMEM((slots, cols), BF16)],
    )
    nears = call(meet_near, [(part, BF16)] * (N_Y - 1), near, got_far)
    (up_far,) = call(meet_far, [(part, BF16)], *got_ups)
    got_nears = [move(g, dy) for dy, g in enumerate(nears, 1)]
    got_up = move(up_far, N_Y)
    got_up, turned = lax.optimization_barrier((got_up, turned))
    parts, loads = call(
        back,
        [((n_blk,) + part, BF16), ((8, COUNT_LANES), jnp.int32)],
        goes_to,
        arrived_cot,
        w_down[0],
        grid=(steps,),
        in_specs=[table, fixed(slots, cols + COUNT_LANES), pl.BlockSpec((TILE, cols), lambda i: (i, 0))],
        out_specs=[tiles(n_blk, chunk, TILE), fixed(8, COUNT_LANES)],
        scratch_shapes=[pltpu.VMEM((slots, cols), BF16)],
        limit=LARGE,
        flops=2 * slots * cols * ff,
        traffic=4_000_000,
    )
    *packs, gate_pre, up_pre = call(
        activate,
        [((2,) + part, BF16)] * n_blk + [(part, F32)] * 2,
        near,
        got_far,
        *got_nears,
        *got_ups,
        got_up,
        parts,
    )
    got = {d: move(packs[d], d) for d in order}
    got = [packs[0]] + [got[d] for d in range(1, n_blk)]
    d_gate, d_up = call(back_act, [(part, BF16)] * 2, gate_pre, up_pre, *got)
    got_dg = move(d_gate, N_Y)
    got_du = [move(d_up, dy) for dy in range(1, N_Y)]
    got, got_dg = lax.optimization_barrier((got, got_dg))
    expert_out, hidden = call(
        expert,
        [((slots, cols), BF16), ((slots, ff), BF16)],
        comes_from,
        w_down[0],
        *got,
        ordered=True,
        limit=LARGE,
        flops=2 * slots * cols * ff,
        traffic=4_000_000,
    )
    returned = to_experts(expert_out, experts)
    dg_pair = jnp.stack([d_gate, got_dg])
    du_four = jnp.stack([d_up] + got_du)
    dg = [dg_pair] + [move(dg_pair, dy) for dy in range(1, N_Y)]
    du = [du_four, move(du_four, N_Y)]
    (grad_down,) = call(
        grad_down_tile,
        [((ff, cols), BF16)],
        hidden,
        arrived_cot,
        grid=(steps,),
        in_specs=[pl.BlockSpec((slots, TILE), lambda i: (0, i)), fixed(slots, cols + COUNT_LANES)],
        out_specs=[pl.BlockSpec((TILE, cols), lambda i: (i, 0))],
        limit=LARGE,
        flops=2 * slots * cols * ff,
        traffic=4_000_000,
    )
    (layer_out,) = call(combine, [((rows, cols), BF16)], gate_hi, gate_lo, returned)
    dg, du, grad_down, layer_out = lax.optimization_barrier((dg, du, grad_down, layer_out))
    grad_gate, grad_up = call(
        grad_tile,
        [((cols, ff), BF16)] * 2,
        turned,
        *dg,
        *du,
        grid=(steps,),
        in_specs=[fixed(cols, slots)] + [tiles(2, chunk, TILE)] * N_Y + [tiles(N_Y, chunk, TILE)] * 2,
        out_specs=[tiles(cols, TILE)] * 2,
        scratch_shapes=[pltpu.VMEM((slots, TILE), BF16)] * 2,
        flops=4 * slots * cols * ff,
        traffic=6_000_000,
    )
    return (layer_out, grad_gate[None], grad_up[None], grad_down[None], loads[:2].reshape(-1))


def solution(mesh):
    return jax.shard_map(
        body,
        mesh=mesh,
        in_specs=(
            P("expert", "blk"),
            P("expert", "blk"),
            P("expert", None),
            P("expert", None),
            P("expert", "blk", None),
            P("expert", "blk", None),
            P("expert", None, "blk"),
        ),
        out_specs=(
            P("expert", "blk"),
            P("expert", "blk", None),
            P("expert", "blk", None),
            P("expert", None, "blk"),
            P(),
        ),
        check_vma=False,
    )
```

time: 272 us -> 177 us (0.65)
  waiting for transfers between devices: 135 us -> 71.8 us
  Pallas kernels: 0 us -> 35.5 us
  blocking collectives: 31.4 us -> 0 us
  starting transfers between devices: 31.2 us -> 62.5 us
  matrix products: 21.7 us -> 0 us
  other arithmetic: 21.2 us -> 0.1 us
  between operations: 14.3 us -> 0.95 us
  local copies, waits for them, and re-layouts: 15.1 us -> 5.21 us
    psum x1 -> x0, waiting for transfers between devices: 91.5 us -> none  [body(): lax.psum(projected.astype(jnp.bfloat16), 'blk').astype(jnp.float32)]
    ppermute x0 -> x23, waiting for transfers between devices: none -> 45.8 us  [move(): return lax.ppermute(array, 'blk', pairs)]
    pallas_call x0 -> x13, Pallas kernels: none -> 35.5 us  [call(): pl.pallas_call(kernel, out_shape=outs, compiler_params=pltpu.CompilerPara...]
    psum x1 -> x0, blocking collectives: 31.4 us -> none  [body(): loads = lax.psum(count_picks(expert_ids), 'expert')]
    ppermute x0 -> x23, starting transfers between devices: none -> 22.4 us  [move(): return lax.ppermute(array, 'blk', pairs)]
    dot_general x9 -> x0, matrix products: 21.7 us -> none  [the longest x3 9.19 us: contract_rows(): lax.dot_general(left, right, (((0,), (0,)), ((), ())), preferred_element_...]
    all_to_all x3, waiting for transfers between devices: 43.2 us -> 26 us  [to_experts(): lax.all_to_all(rows.reshape(experts, CAP, cols), 'expert', split_axis=0,...]
    another operation x4 -> x2, other arithmetic: 10.9 us -> 0.1 us  [the longest x1 0.07 us: body(): du_four = jnp.stack([d_up] + got_du)]
  transfers between devices with their start and end apart: 4 -> 26, of which waited for: 3 -> 16; matrix products, arithmetic and copies ran while one was open for 6% -> 1% of each run, Pallas kernels for 0% -> 13%
where the time goes in v1:
time: 177 us; the launch traced here: 176 us
  waiting for transfers between devices  71.8 us (41%)
  starting transfers between devices  62.5 us (35%)
  Pallas kernels  35.5 us (20%)
  local copies, waits for them, and re-layouts  5.21 us (3%)
    ppermute x23, waiting for transfers between devices, move(): return lax.ppermute(array, 'blk', pairs)  45.8 us
    all_to_all x3, starting transfers between devices, to_experts(): lax.all_to_all(rows.reshape(experts, CAP, cols), 'expert', split_axis=0,...  40.1 us
    pallas_call x13, Pallas kernels, call(): pl.pallas_call(kernel, out_shape=outs, compiler_params=pltpu.CompilerPara...  35.5 us
    all_to_all x3, waiting for transfers between devices, to_experts(): lax.all_to_all(rows.reshape(experts, CAP, cols), 'expert', split_axis=0,...  26 us
    ppermute x23, starting transfers between devices, move(): return lax.ppermute(array, 'blk', pairs)  22.4 us
  transfers between devices with their start and end apart: 26, of which 16 were waited for; matrix products, arithmetic and copies ran while one was open for 1% of the time, Pallas kernels for 13%

profile of v1, /device:TPU:1, one launch (start us, length us, event | category | flops | bytes accessed | tf_op | source)
XLA Modules:
  0.0 176.0 jit_solution(7989517436481845029)
XLA Ops:
  0.6 2.7 %route.1 = bf16[512,896]{1,0:T(8,128)(2,1)} custom-call(s32[8,256]{1,0:T(8,128)} %bitcast.45, bf16[256,896]{1,0:T(8,128)(2,1)} %tok_ref.1), custom_call_target="tpu_custom_call" | custom-call | tf_op jit(solution)/shard_map/route/pallas_call | solution.py:55
  3.3 12.6 %all-to-all-start = ((bf16[32,16,896]{2,1,0:T(8,128)(2,1)}), bf16[32,16,896]{2,1,0:T(8,128)(2,1)S(1)}, u32[]{:S(2)}, u32[]{:S(2)}) async-start(bf16[32,16,896]{2,1,0:T(8,128)(2,1)} %bitcast.35), calls=%async_computation | async-start | bytes 1835008 | tf_op jit(solution)/shard_map/all_to_all | solution.py:240
  16.6 3.2 %route_back.1 = (bf16[512,1024]{1,0:T(8,128)(2,1)}, bf16[256,512]{1,0:T(8,128)(2,1)}, bf16[256,512]{1,0:T(8,128)(2,1)}) custom-call(s32[8,256]{1,0:T(8,128)} %bitcast.46, s32[8,256]{1,0:T(8,128)} %bitcast.47, bf16[256,896]{1,0:T(8,128)(2,1)} %cot_ref.1), custom_call_target="tpu_custom_call" | custom-call | tf_op jit(solution)/shard_map/route_back/pallas_call | solution.py:55
  19.8 21.1 %all-to-all-done = bf16[32,16,896]{2,1,0:T(8,128)(2,1)S(1)} async-done(((bf16[32,16,896]{2,1,0:T(8,128)(2,1)}), bf16[32,16,896]{2,1,0:T(8,128)(2,1)S(1)}, u32[]{:S(2)}, u32[]{:S(2)}) %all-to-all-start) | async-done | bytes 917536 | tf_op jit(solution)/shard_map/all_to_all | solution.py:240
  40.9 6.9 %all-to-all-start.1 = ((bf16[32,16,1024]{2,1,0:T(8,128)(2,1)}), bf16[32,16,1024]{2,1,0:T(8,128)(2,1)}, u32[]{:S(2)}, u32[]{:S(2)}) async-start(bf16[32,16,1024]{2,1,0:T(8,128)(2,1)} %bitcast.39), calls=%async_computation.1 | async-start | bytes 2097152 | tf_op jit(solution)/shard_map/all_to_all | solution.py:240
  47.8 5.9 %project.1 = (bf16[4,64,1024]{2,1,0:T(8,128)(2,1)}, bf16[4,64,1024]{2,1,0:T(8,128)(2,1)}, bf16[2,64,1024]{2,1,0:T(8,128)(2,1)}, bf16[2,64,1024]{2,1,0:T(8,128)(2...) custom-call(s32[8]{0:T(128)} %stack.70.order_ref, bf16[512,896]{1,0:T(8,128)(2,1)} %bitcast.30, ...), custom_call_target="tpu_custom_call" | custom-call | flops 1879048192 | bytes 7000000 | tf_op jit(solution)/shard_map/project/pallas_call | solution.py:55
  55.4 2.6 %collective-permute-start.5 = (bf16[2,64,1024]{2,1,0:T(8,128)(2,1)}, bf16[2,64,1024]{2,1,0:T(8,128)(2,1)S(1)}, u32[]{:S(2)}, u32[]{:S(2)}) collective-permute-start(bf16[2,64,1024]{2,1,0:T(8,128)(2,1)} %get-tuple-element.66), channel_id=1, source_target_pairs={{0,2},{1,3},{2,0},{3,1},{4,6},{5,7},{6,4},{7,5},{8,10},{9,11},{10,... | collective-permute-start | bytes 786440 | tf_op jit(solution)/shard_map/ppermute | solution.py:235
  59.1 3.8 %collective-permute-done.4.refs_1_.u1 = bf16[2,64,1024]{2,1,0:T(8,128)(2,1)S(1)} collective-permute-done((bf16[2,64,1024]{2,1,0:T(8,128)(2,1)}, bf16[2,64,1024]{2,1,0:T(8,128)(2,1)S(1)}, u32[]{:S(2)}, u32[]{:S(2)}) %collective-permute-start.4) | collective-permute-done | bytes 262176 | tf_op jit(solution)/shard_map/ppermute | solution.py:235
  62.9 6.7 %collective-permute-done.5.refs_2_.u2 = bf16[2,64,1024]{2,1,0:T(8,128)(2,1)S(1)} collective-permute-done((bf16[2,64,1024]{2,1,0:T(8,128)(2,1)}, bf16[2,64,1024]{2,1,0:T(8,128)(2,1)S(1)}, u32[]{:S(2)}, u32[]{:S(2)}) %collective-permute-start.5) | collective-permute-done | bytes 262176 | tf_op jit(solution)/shard_map/ppermute | solution.py:235
  77.8 2.6 %collective-permute-start.2 = (bf16[64,1024]{1,0:T(8,128)(2,1)}, bf16[64,1024]{1,0:T(8,128)(2,1)S(1)}, u32[]{:S(2)}, u32[]{:S(2)}) collective-permute-start(bf16[64,1024]{1,0:T(8,128)(2,1)} %get-tuple-element.62), channel_id=1, source_target_pairs={{0,2},{1,3},{2,0},{3,1},{4,6},{5,7},{6,4},{7,5},{8,10},{9,11},{10,... | collective-permute-start | bytes 393224 | tf_op jit(solution)/shard_map/ppermute | solution.py:235
  82.4 5.1 %back.1 = (bf16[8,64,1024]{2,1,0:T(8,128)(2,1)}, s32[8,128]{1,0:T(8,128)}) custom-call(s32[8]{0:T(128)} %stack.70.order_ref, bf16[512,1024]{1,0:T(8,128)(2,1)} %bitcast.15.c_ref, bf16[1024,896]{1,0:T(8,128)(2,1)} %bitcast.36), custom_call_target="tpu_custom_call" | custom-call | flops 939524096 | bytes 4000000 | tf_op jit(solution)/shard_map/back/pallas_call | solution.py:55
  93.5 3.9 %collective-permute-done.8.rest_1_ = bf16[2,64,1024]{2,1,0:T(8,128)(2,1)S(1)} collective-permute-done((bf16[2,64,1024]{2,1,0:T(8,128)(2,1)S(1)}, bf16[2,64,1024]{2,1,0:T(8,128)(2,1)S(1)}, u32[]{:S(2)}, u32[]{:S(2)}) %collective-permute-start.8) | collective-permute-done | bytes 262176 | tf_op jit(solution)/shard_map/ppermute | solution.py:235
  97.4 4.9 %collective-permute-done.9.rest_2_ = bf16[2,64,1024]{2,1,0:T(8,128)(2,1)S(1)} collective-permute-done((bf16[2,64,1024]{2,1,0:T(8,128)(2,1)S(1)}, bf16[2,64,1024]{2,1,0:T(8,128)(2,1)S(1)}, u32[]{:S(2)}, u32[]{:S(2)}) %collective-permute-start.9) | collective-permute-done | bytes 262176 | tf_op jit(solution)/shard_map/ppermute | solution.py:235
  102.3 2.3 %collective-permute-done.10.rest_3_ = bf16[2,64,1024]{2,1,0:T(8,128)(2,1)S(1)} collective-permute-done((bf16[2,64,1024]{2,1,0:T(8,128)(2,1)S(1)}, bf16[2,64,1024]{2,1,0:T(8,128)(2,1)S(1)}, u32[]{:S(2)}, u32[]{:S(2)}) %collective-permute-start.10) | collective-permute-done | bytes 262176 | tf_op jit(solution)/shard_map/ppermute | solution.py:235
  104.6 5.3 %collective-permute-done.13.rest_6_ = bf16[2,64,1024]{2,1,0:T(8,128)(2,1)S(1)} collective-permute-done((bf16[2,64,1024]{2,1,0:T(8,128)(2,1)S(1)}, bf16[2,64,1024]{2,1,0:T(8,128)(2,1)S(1)}, u32[]{:S(2)}, u32[]{:S(2)}) %collective-permute-start.13) | collective-permute-done | bytes 262176 | tf_op jit(solution)/shard_map/ppermute | solution.py:235
  113.2 3.4 %collective-permute-done.15 = bf16[64,1024]{1,0:T(8,128)(2,1)S(1)} collective-permute-done((bf16[64,1024]{1,0:T(8,128)(2,1)S(1)}, bf16[64,1024]{1,0:T(8,128)(2,1)S(1)}, u32[]{:S(2)}, u32[]{:S(2)}) %collective-permute-start.15) | collective-permute-done | bytes 131104 | tf_op jit(solution)/shard_map/ppermute | solution.py:235
  116.6 4.3 %expert.1 = (bf16[512,896]{1,0:T(8,128)(2,1)}, bf16[512,1024]{1,0:T(8,128)(2,1)}) custom-call(s32[8]{0:T(128)} %copy-done.17, bf16[1024,896]{1,0:T(8,128)(2,1)} %bitcast.37, bf16[2,64,1024]{2,1,0:T(8,128)(2,1)} %copy-done.7, bf16[2,64,1024]{2,1,0:T(8,128)(2,1)} %copy-done.8, bf16[2,64,1024]{2,1,0:T(8,128)(2,1)} %copy-done.9, ...), custom_call_target="tpu_custom_call" | custom-call | flops 939524096 | bytes 4000000 | tf_op jit(solution)/shard_map/expert/pallas_call | solution.py:55
  120.9 20.7 %all-to-all-start.2 = ((bf16[32,16,896]{2,1,0:T(8,128)(2,1)}), bf16[32,16,896]{2,1,0:T(8,128)(2,1)S(1)}, u32[]{:S(2)}, u32[]{:S(2)}) async-start(bf16[32,16,896]{2,1,0:T(8,128)(2,1)} %bitcast.40), calls=%async_computation.2 | async-start | bytes 1835008 | tf_op jit(solution)/shard_map/all_to_all | solution.py:240
  141.6 2.5 %collective-permute-start.21 = (bf16[64,1024]{1,0:T(8,128)(2,1)S(1)}, bf16[64,1024]{1,0:T(8,128)(2,1)S(1)}, u32[]{:S(2)}, u32[]{:S(2)}) collective-permute-start(bf16[64,1024]{1,0:T(8,128)(2,1)S(1)} %get-tuple-element.84), channel_id=1, source_target_pairs={{0,3},{1,0},{2,1},{3,2},{4,7},{5,4},{6,5},{7,6},{8,11},{9,8},{10,9... | collective-permute-start | bytes 393224 | tf_op jit(solution)/shard_map/ppermute | solution.py:235
  144.8 4.6 %collective-permute-done.21 = bf16[64,1024]{1,0:T(8,128)(2,1)S(1)} collective-permute-done((bf16[64,1024]{1,0:T(8,128)(2,1)S(1)}, bf16[64,1024]{1,0:T(8,128)(2,1)S(1)}, u32[]{:S(2)}, u32[]{:S(2)}) %collective-permute-start.21) | collective-permute-done | bytes 131104 | tf_op jit(solution)/shard_map/ppermute | solution.py:235
  150.1 3.7 %collective-permute-done.19 = bf16[64,1024]{1,0:T(8,128)(2,1)S(1)} collective-permute-done((bf16[64,1024]{1,0:T(8,128)(2,1)S(1)}, bf16[64,1024]{1,0:T(8,128)(2,1)S(1)}, u32[]{:S(2)}, u32[]{:S(2)}) %collective-permute-start.19) | collective-permute-done | bytes 131104 | tf_op jit(solution)/shard_map/ppermute | solution.py:235
  157.0 4.8 %grad_down_tile.1 = bf16[1024,896]{1,0:T(8,128)(2,1)} custom-call(bf16[512,1024]{1,0:T(8,128)(2,1)} %get-tuple-element.93.hidden_ref, bf16[512,1024]{1,0:T(8,128)(2,1)} %bitcast.15.c_ref), custom_call_target="tpu_custom_call" | custom-call | flops 939524096 | bytes 4000000 | tf_op jit(solution)/shard_map/grad_down_tile/pallas_call | solution.py:55
  161.7 4.9 %all-to-all-done.2 = bf16[32,16,896]{2,1,0:T(8,128)(2,1)S(1)} async-done(((bf16[32,16,896]{2,1,0:T(8,128)(2,1)}), bf16[32,16,896]{2,1,0:T(8,128)(2,1)S(1)}, u32[]{:S(2)}, u32[]{:S(2)}) %all-to-all-start.2) | async-done | bytes 917536 | tf_op jit(solution)/shard_map/all_to_all | solution.py:240
  170.7 5.2 %grad_tile.1 = (bf16[896,1024]{1,0:T(8,128)(2,1)}, bf16[896,1024]{1,0:T(8,128)(2,1)}) custom-call(bf16[896,512]{1,0:T(8,128)(2,1)S(1)} %turn.1.x_ref, bf16[2,64,1024]{2,1,0:T(8,128)(2,1)S(1)} %pad_maximum_fusion.1.g0, bf16[2,64,1024]{2,1,0:T(8,128)(2,1)} %collective-permute-done.16.g1, bf16[2,64,1024]{2,1,0:T(8,128)(2,1)} %collective-permute-done.17.g2, ...), custom_call_target="tpu_custom_call" | custom-call | flops 1879048192 | bytes 6000000 | tf_op jit(solution)/shard_map/grad_tile/pallas_call | solution.py:55
  (82 shorter events, 31.6 us)
Async XLA Ops:
  3.3 37.6 %all-to-all-start = ((bf16[32,16,896]{2,1,0:T(8,128)(2,1)}), bf16[32,16,896]{2,1,0:T(8,128)(2,1)S(1)}, u32[]{:S(2)}, u32[]{:S(2)}) async-start(bf16[32,16,896]{2,1,0:T(8,128)(2,1)} %bitcast.35), calls=%async_computation | async-start | bytes 1835008 | tf_op jit(solution)/shard_map/all_to_all | solution.py:240
  40.9 41.4 %all-to-all-start.1 = ((bf16[32,16,1024]{2,1,0:T(8,128)(2,1)}), bf16[32,16,1024]{2,1,0:T(8,128)(2,1)}, u32[]{:S(2)}, u32[]{:S(2)}) async-start(bf16[32,16,1024]{2,1,0:T(8,128)(2,1)} %bitcast.39), calls=%async_computation.1 | async-start | bytes 2097152 | tf_op jit(solution)/shard_map/all_to_all | solution.py:240
  53.7 21.0 %collective-permute-start = (bf16[4,64,1024]{2,1,0:T(8,128)(2,1)}, bf16[4,64,1024]{2,1,0:T(8,128)(2,1)S(1)}, u32[]{:S(2)}, u32[]{:S(2)}) collective-permute-start(bf16[4,64,1024]{2,1,0:T(8,128)(2,1)} %get-tuple-element.60), channel_id=1, source_target_pairs={{0,4},{1,5},{2,6},{3,7},{4,0},{5,1},{6,2},{7,3},{8,12},{9,13},{10,... | collective-permute-start | bytes 1572872 | tf_op jit(solution)/shard_map/ppermute | solution.py:235
  54.1 8.8 %collective-permute-start.4 = (bf16[2,64,1024]{2,1,0:T(8,128)(2,1)}, bf16[2,64,1024]{2,1,0:T(8,128)(2,1)S(1)}, u32[]{:S(2)}, u32[]{:S(2)}) collective-permute-start(bf16[2,64,1024]{2,1,0:T(8,128)(2,1)} %get-tuple-element.65), channel_id=1, source_target_pairs={{0,1},{1,2},{2,3},{3,0},{4,5},{5,6},{6,7},{7,4},{8,9},{9,10},{10,1... | collective-permute-start | bytes 786440 | tf_op jit(solution)/shard_map/ppermute | solution.py:235
  55.4 14.2 %collective-permute-start.5 = (bf16[2,64,1024]{2,1,0:T(8,128)(2,1)}, bf16[2,64,1024]{2,1,0:T(8,128)(2,1)S(1)}, u32[]{:S(2)}, u32[]{:S(2)}) collective-permute-start(bf16[2,64,1024]{2,1,0:T(8,128)(2,1)} %get-tuple-element.66), channel_id=1, source_target_pairs={{0,2},{1,3},{2,0},{3,1},{4,6},{5,7},{6,4},{7,5},{8,10},{9,11},{10,... | collective-permute-start | bytes 786440 | tf_op jit(solution)/shard_map/ppermute | solution.py:235
  58.0 11.6 %collective-permute-start.6 = (bf16[2,64,1024]{2,1,0:T(8,128)(2,1)}, bf16[2,64,1024]{2,1,0:T(8,128)(2,1)S(1)}, u32[]{:S(2)}, u32[]{:S(2)}) collective-permute-start(bf16[2,64,1024]{2,1,0:T(8,128)(2,1)} %get-tuple-element.67), channel_id=1, source_target_pairs={{0,3},{1,0},{2,1},{3,2},{4,7},{5,4},{6,5},{7,6},{8,11},{9,8},{10,9... | collective-permute-start | bytes 786440 | tf_op jit(solution)/shard_map/ppermute | solution.py:235
  71.3 16.2 %collective-permute-start.7 = (bf16[64,1024]{1,0:T(8,128)(2,1)}, bf16[64,1024]{1,0:T(8,128)(2,1)S(1)}, u32[]{:S(2)}, u32[]{:S(2)}) collective-permute-start(bf16[64,1024]{1,0:T(8,128)(2,1)} %meet_far.1), channel_id=1, source_target_pairs={{0,4},{1,5},{2,6},{3,7},{4,0},{5,1},{6,2},{7,3},{8,12},{9,13},{10,... | collective-permute-start | bytes 393224 | tf_op jit(solution)/shard_map/ppermute | solution.py:235
  76.5 11.0 %collective-permute-start.1 = (bf16[64,1024]{1,0:T(8,128)(2,1)}, bf16[64,1024]{1,0:T(8,128)(2,1)S(1)}, u32[]{:S(2)}, u32[]{:S(2)}) collective-permute-start(bf16[64,1024]{1,0:T(8,128)(2,1)} %get-tuple-element.61), channel_id=1, source_target_pairs={{0,1},{1,2},{2,3},{3,0},{4,5},{5,6},{6,7},{7,4},{8,9},{9,10},{10,1... | collective-permute-start | bytes 393224 | tf_op jit(solution)/shard_map/ppermute | solution.py:235
  77.8 9.7 %collective-permute-start.2 = (bf16[64,1024]{1,0:T(8,128)(2,1)}, bf16[64,1024]{1,0:T(8,128)(2,1)S(1)}, u32[]{:S(2)}, u32[]{:S(2)}) collective-permute-start(bf16[64,1024]{1,0:T(8,128)(2,1)} %get-tuple-element.62), channel_id=1, source_target_pairs={{0,2},{1,3},{2,0},{3,1},{4,6},{5,7},{6,4},{7,5},{8,10},{9,11},{10,... | collective-permute-start | bytes 393224 | tf_op jit(solution)/shard_map/ppermute | solution.py:235
  80.4 7.0 %collective-permute-start.3 = (bf16[64,1024]{1,0:T(8,128)(2,1)}, bf16[64,1024]{1,0:T(8,128)(2,1)S(1)}, u32[]{:S(2)}, u32[]{:S(2)}) collective-permute-start(bf16[64,1024]{1,0:T(8,128)(2,1)} %get-tuple-element.63), channel_id=1, source_target_pairs={{0,3},{1,0},{2,1},{3,2},{4,7},{5,4},{6,5},{7,6},{8,11},{9,8},{10,9... | collective-permute-start | bytes 393224 | tf_op jit(solution)/shard_map/ppermute | solution.py:235
  89.0 8.4 %collective-permute-start.8 = (bf16[2,64,1024]{2,1,0:T(8,128)(2,1)S(1)}, bf16[2,64,1024]{2,1,0:T(8,128)(2,1)S(1)}, u32[]{:S(2)}, u32[]{:S(2)}) collective-permute-start(bf16[2,64,1024]{2,1,0:T(8,128)(2,1)S(1)} %get-tuple-element.75), channel_id=1, source_target_pairs={{0,1},{1,2},{2,3},{3,0},{4,5},{5,6},{6,7},{7,4},{8,9},{9,10},{10,1... | collective-permute-start | bytes 786440 | tf_op jit(solution)/shard_map/ppermute | solution.py:235
  89.5 12.8 %collective-permute-start.9 = (bf16[2,64,1024]{2,1,0:T(8,128)(2,1)S(1)}, bf16[2,64,1024]{2,1,0:T(8,128)(2,1)S(1)}, u32[]{:S(2)}, u32[]{:S(2)}) collective-permute-start(bf16[2,64,1024]{2,1,0:T(8,128)(2,1)S(1)} %get-tuple-element.76), channel_id=1, source_target_pairs={{0,2},{1,3},{2,0},{3,1},{4,6},{5,7},{6,4},{7,5},{8,10},{9,11},{10,... | collective-permute-start | bytes 786440 | tf_op jit(solution)/shard_map/ppermute | solution.py:235
  90.8 13.8 %collective-permute-start.10 = (bf16[2,64,1024]{2,1,0:T(8,128)(2,1)S(1)}, bf16[2,64,1024]{2,1,0:T(8,128)(2,1)S(1)}, u32[]{:S(2)}, u32[]{:S(2)}) collective-permute-start(bf16[2,64,1024]{2,1,0:T(8,128)(2,1)S(1)} %get-tuple-element.77), channel_id=1, source_target_pairs={{0,3},{1,0},{2,1},{3,2},{4,7},{5,4},{6,5},{7,6},{8,11},{9,8},{10,9... | collective-permute-start | bytes 786440 | tf_op jit(solution)/shard_map/ppermute | solution.py:235
  92.0 12.6 %collective-permute-start.11 = (bf16[2,64,1024]{2,1,0:T(8,128)(2,1)S(1)}, bf16[2,64,1024]{2,1,0:T(8,128)(2,1)S(1)}, u32[]{:S(2)}, u32[]{:S(2)}) collective-permute-start(bf16[2,64,1024]{2,1,0:T(8,128)(2,1)S(1)} %get-tuple-element.78), channel_id=1, source_target_pairs={{0,4},{1,5},{2,6},{3,7},{4,0},{5,1},{6,2},{7,3},{8,12},{9,13},{10,... | collective-permute-start | bytes 786440 | tf_op jit(solution)/shard_map/ppermute | solution.py:235
  92.8 11.8 %collective-permute-start.12 = (bf16[2,64,1024]{2,1,0:T(8,128)(2,1)S(1)}, bf16[2,64,1024]{2,1,0:T(8,128)(2,1)S(1)}, u32[]{:S(2)}, u32[]{:S(2)}) collective-permute-start(bf16[2,64,1024]{2,1,0:T(8,128)(2,1)S(1)} %get-tuple-element.79), channel_id=1, source_target_pairs={{0,5},{1,6},{2,7},{3,4},{4,1},{5,2},{6,3},{7,0},{8,13},{9,14},{10,... | collective-permute-start | bytes 786440 | tf_op jit(solution)/shard_map/ppermute | solution.py:235
  97.4 12.5 %collective-permute-start.13 = (bf16[2,64,1024]{2,1,0:T(8,128)(2,1)S(1)}, bf16[2,64,1024]{2,1,0:T(8,128)(2,1)S(1)}, u32[]{:S(2)}, u32[]{:S(2)}) collective-permute-start(bf16[2,64,1024]{2,1,0:T(8,128)(2,1)S(1)} %get-tuple-element.80), channel_id=1, source_target_pairs={{0,6},{1,7},{2,4},{3,5},{4,2},{5,3},{6,0},{7,1},{8,14},{9,15},{10,... | collective-permute-start | bytes 786440 | tf_op jit(solution)/shard_map/ppermute | solution.py:235
  102.3 9.3 %collective-permute-start.14 = (bf16[2,64,1024]{2,1,0:T(8,128)(2,1)S(1)}, bf16[2,64,1024]{2,1,0:T(8,128)(2,1)S(1)}, u32[]{:S(2)}, u32[]{:S(2)}) collective-permute-start(bf16[2,64,1024]{2,1,0:T(8,128)(2,1)S(1)} %get-tuple-element.81), channel_id=1, source_target_pairs={{0,7},{1,4},{2,5},{3,6},{4,3},{5,0},{6,1},{7,2},{8,15},{9,12},{10,... | collective-permute-start | bytes 786440 | tf_op jit(solution)/shard_map/ppermute | solution.py:235
  120.9 45.7 %all-to-all-start.2 = ((bf16[32,16,896]{2,1,0:T(8,128)(2,1)}), bf16[32,16,896]{2,1,0:T(8,128)(2,1)S(1)}, u32[]{:S(2)}, u32[]{:S(2)}) async-start(bf16[32,16,896]{2,1,0:T(8,128)(2,1)} %bitcast.40), calls=%async_computation.2 | async-start | bytes 1835008 | tf_op jit(solution)/shard_map/all_to_all | solution.py:240
  141.6 7.8 %collective-permute-start.21 = (bf16[64,1024]{1,0:T(8,128)(2,1)S(1)}, bf16[64,1024]{1,0:T(8,128)(2,1)S(1)}, u32[]{:S(2)}, u32[]{:S(2)}) collective-permute-start(bf16[64,1024]{1,0:T(8,128)(2,1)S(1)} %get-tuple-element.84), channel_id=1, source_target_pairs={{0,3},{1,0},{2,1},{3,2},{4,7},{5,4},{6,5},{7,6},{8,11},{9,8},{10,9... | collective-permute-start | bytes 393224 | tf_op jit(solution)/shard_map/ppermute | solution.py:235
  144.8 9.0 %collective-permute-start.19 = (bf16[64,1024]{1,0:T(8,128)(2,1)S(1)}, bf16[64,1024]{1,0:T(8,128)(2,1)S(1)}, u32[]{:S(2)}, u32[]{:S(2)}) collective-permute-start(bf16[64,1024]{1,0:T(8,128)(2,1)S(1)} %get-tuple-element.84), channel_id=1, source_target_pairs={{0,1},{1,2},{2,3},{3,0},{4,5},{5,6},{6,7},{7,4},{8,9},{9,10},{10,1... | collective-permute-start | bytes 393224 | tf_op jit(solution)/shard_map/ppermute | solution.py:235
  153.9 16.9 %collective-permute-start.22 = (bf16[4,64,1024]{2,1,0:T(8,128)(2,1)S(1)}, bf16[4,64,1024]{2,1,0:T(8,128)(2,1)}, u32[]{:S(2)}, u32[]{:S(2)}) collective-permute-start(bf16[4,64,1024]{2,1,0:T(8,128)(2,1)S(1)} %pad_maximum_fusion.u0), channel_id=1, source_target_pairs={{0,4},{1,5},{2,6},{3,7},{4,0},{5,1},{6,2},{7,3},{8,12},{9,13},{10,... | collective-permute-start | bytes 1572872 | tf_op jit(solution)/shard_map/ppermute | solution.py:235
  154.0 14.1 %collective-permute-start.18 = (bf16[2,64,1024]{2,1,0:T(8,128)(2,1)S(1)}, bf16[2,64,1024]{2,1,0:T(8,128)(2,1)S(1)}, u32[]{:S(2)}, u32[]{:S(2)}) collective-permute-start(bf16[2,64,1024]{2,1,0:T(8,128)(2,1)S(1)} %pad_maximum_fusion.1.g0), channel_id=1, source_target_pairs={{0,3},{1,0},{2,1},{3,2},{4,7},{5,4},{6,5},{7,6},{8,11},{9,8},{10,9... | collective-permute-start | bytes 786440 | tf_op jit(solution)/shard_map/ppermute | solution.py:235
  154.1 14.1 %collective-permute-start.17 = (bf16[2,64,1024]{2,1,0:T(8,128)(2,1)S(1)}, bf16[2,64,1024]{2,1,0:T(8,128)(2,1)}, u32[]{:S(2)}, u32[]{:S(2)}) collective-permute-start(bf16[2,64,1024]{2,1,0:T(8,128)(2,1)S(1)} %pad_maximum_fusion.1.g0), channel_id=1, source_target_pairs={{0,2},{1,3},{2,0},{3,1},{4,6},{5,7},{6,4},{7,5},{8,10},{9,11},{10,... | collective-permute-start | bytes 786440 | tf_op jit(solution)/shard_map/ppermute | solution.py:235
  154.9 14.7 %collective-permute-start.16 = (bf16[2,64,1024]{2,1,0:T(8,128)(2,1)S(1)}, bf16[2,64,1024]{2,1,0:T(8,128)(2,1)}, u32[]{:S(2)}, u32[]{:S(2)}) collective-permute-start(bf16[2,64,1024]{2,1,0:T(8,128)(2,1)S(1)} %pad_maximum_fusion.1.g0), channel_id=1, source_target_pairs={{0,1},{1,2},{2,3},{3,0},{4,5},{5,6},{6,7},{7,4},{8,9},{9,10},{10,1... | collective-permute-start | bytes 786440 | tf_op jit(solution)/shard_map/ppermute | solution.py:235
  (20 other events, 252.2 us)

commit v2 on v1

--- a/solution.py
+++ b/solution.py
@@ -9,7 +9,8 @@
 TOPK = 8
 CAP = 16
 N_Y = 4
-TILE = 256
+TILE = 512
+NEAR = 384
 F32 = jnp.float32
 BF16 = jnp.bfloat16
 MIB = 1024 * 1024
@@ -133,7 +134,7 @@
 
 
 def project(order_ref, x_ref, wg_ref, wu_ref, far_ref, near_ref, *rest):
-    ups, held = rest[:-1], rest[-1]
+    wides, held = rest[:-1], rest[-1]
     chunk = far_ref.shape[1]
     in_order(order_ref, x_ref, held)
     gate = matmul(held[...], wg_ref[...]).astype(BF16)
@@ -141,8 +142,9 @@
     for dx in range(2):
         for dy in range(N_Y):
             at = (dx * N_Y + dy) * chunk
-            (near_ref, far_ref)[dx][dy] = gate[at : at + chunk]
-            ups[dy][dx] = up[at : at + chunk]
+            (near_ref, far_ref)[dx][dy] = gate[at : at + chunk, :NEAR]
+            wides[dy][dx, :, : TILE - NEAR] = gate[at : at + chunk, NEAR:]
+            wides[dy][dx, :, TILE - NEAR :] = up[at : at + chunk]
 
 
 def meet_near(near_ref, got_ref, *outs):
@@ -155,27 +157,31 @@
     out[...] = sum(r[1].astype(F32) for r in refs[:-1]).astype(BF16)
 
 
-def activate(near_ref, got_ref, g1, g2, g3, u0, u1, u2, u3, got_u, part_ref, *rest):
-    outs, (gate_ref, up_ref) = rest[:-2], rest[-2:]
-    gate = near_ref[0].astype(F32) + got_ref[0].astype(F32)
-    for r in (g1, g2, g3):
-        gate = gate + r[...].astype(F32)
-    up = got_u[...].astype(F32)
-    for r in (u0, u1, u2, u3):
-        up = up + r[0].astype(F32)
-    gate_ref[...] = gate
-    up_ref[...] = up
-    hidden = (gate * jax.nn.sigmoid(gate) * up).astype(BF16)
-    for d, out in enumerate(outs):
-        out[0] = hidden
-        out[1] = part_ref[d]
-
-
-def back(order_ref, c_ref, w_ref, part_ref, load_ref, held):
-    slots, cols = held.shape
+def activate(near_ref, got_ref, n1, n2, n3, w0, w1, w2, w3, got_w, part_ref, pack_ref, gate_ref, up_ref):
+    near = near_ref[0].astype(F32) + got_ref[0].astype(F32)
+    for r in (n1, n2, n3):
+        near = near + r[...].astype(F32)
+    wide = got_w[...].astype(F32)
+    for r in (w0, w1, w2, w3):
+        wide = wide + r[0].astype(F32)
+    span = 2 * TILE - NEAR
+    for i in range(gate_ref.shape[1] // TILE):
+        gate_ref[:, i * TILE : i * TILE + NEAR] = near[:, i * NEAR : (i + 1) * NEAR]
+        gate_ref[:, i * TILE + NEAR : (i + 1) * TILE] = wide[:, i * span : i * span + TILE - NEAR]
+        up_ref[:, i * TILE : (i + 1) * TILE] = wide[:, i * span + TILE - NEAR : (i + 1) * span]
+    gate = gate_ref[...]
+    hidden = (gate * jax.nn.sigmoid(gate) * up_ref[...]).astype(BF16)
+    chunk = hidden.shape[0]
+    for d in range(pack_ref.shape[0]):
+        pack_ref[d, :chunk] = hidden
+        pack_ref[d, chunk:] = part_ref[d]
+
+
+def back(c_ref, w_ref, part_ref, load_ref):
+    slots = c_ref.shape[0]
+    cols = w_ref.shape[1]
     chunk = part_ref.shape[1]
-    in_order(order_ref, c_ref, held)
-    partial = dot(held[...], w_ref[...], ((1,), (1,))).astype(BF16)
+    partial = dot(c_ref[:, :cols], w_ref[...], ((1,), (1,))).astype(BF16)
     for d in range(part_ref.shape[0]):
         part_ref[d] = partial[d * chunk : (d + 1) * chunk]
 
@@ -185,17 +191,17 @@
         load_ref[...] = matmul(counted, c_ref[:, cols:]).astype(jnp.int32)
 
 
-def expert(order_ref, w_ref, *rest):
-    pieces, (out_ref, hidden_ref) = rest[:-2], rest[-2:]
-    chunk = pieces[0].shape[1]
-    for d, piece in enumerate(pieces):
-        hidden_ref[rows_of(order_ref, d, chunk), :] = piece[0]
+def expert(w_ref, got_ref, out_ref, hidden_ref):
+    n, chunk = got_ref.shape[0], got_ref.shape[1]
+    for d in range(n):
+        hidden_ref[d * chunk : (d + 1) * chunk, :] = got_ref[d]
     out_ref[...] = matmul(hidden_ref[...], w_ref[...]).astype(BF16)
 
 
-def back_act(gate_ref, up_ref, *rest):
-    parts, (dg_ref, du_ref) = rest[:-2], rest[-2:]
-    d = sum(r[1].astype(F32) for r in parts)
+def back_act(gate_ref, up_ref, part_ref, dg_ref, du_ref):
+    d = part_ref[0].astype(F32)
+    for i in range(1, part_ref.shape[0]):
+        d = d + part_ref[i].astype(F32)
     gate = gate_ref[...]
     sigma = jax.nn.sigmoid(gate)
     dg_ref[...] = (d * up_ref[...] * sigma * (1.0 + gate * (1.0 - sigma))).astype(BF16)
@@ -254,7 +260,7 @@
     ids = expert_ids.T
     part = (chunk, ff)
 
-    order = (4, 1, 3, 2, 5, 6, 7)
+    order = (3, 4, 1, 2, 5, 6, 7)
 
     def tiles(*block):
         zeros = (0,) * (len(block) - 1)
@@ -276,17 +282,18 @@
         limit=LARGE,
     )
     routed_cot, goes_to, comes_from = lax.optimization_barrier((routed_cot, goes_to, comes_from))
-    shapes = [(N_Y, chunk)] * 2 + [(2, chunk)] * N_Y
+    span = 2 * TILE - NEAR
+    shapes = [(N_Y, chunk, NEAR)] * 2 + [(2, chunk, span)] * N_Y
     far, near, *ups = call(
         project,
-        [(a + (ff,), BF16) for a in shapes],
+        [(a[:2] + (a[2] * steps,), BF16) for a in shapes],
         goes_to,
         arrived,
         w_gate[0],
         w_up[0],
         grid=(steps,),
         in_specs=[table, fixed(slots, cols), tiles(cols, TILE), tiles(cols, TILE)],
-        out_specs=[tiles(*a, TILE) for a in shapes],
+        out_specs=[tiles(*a) for a in shapes],
         scratch_shapes=[pltpu.VMEM((slots, cols), BF16)],
         limit=LARGE,
         flops=4 * slots * cols * ff,
@@ -304,28 +311,25 @@
         ordered=True,
         scratch_shapes=[pltpu.VMEM((slots, cols), BF16)],
     )
-    nears = call(meet_near, [(part, BF16)] * (N_Y - 1), near, got_far)
-    (up_far,) = call(meet_far, [(part, BF16)], *got_ups)
+    nears = call(meet_near, [((chunk, NEAR * steps), BF16)] * (N_Y - 1), near, got_far)
+    (up_far,) = call(meet_far, [((chunk, span * steps), BF16)], *got_ups)
     got_nears = [move(g, dy) for dy, g in enumerate(nears, 1)]
     got_up = move(up_far, N_Y)
-    got_up, turned = lax.optimization_barrier((got_up, turned))
     parts, loads = call(
         back,
         [((n_blk,) + part, BF16), ((8, COUNT_LANES), jnp.int32)],
-        goes_to,
         arrived_cot,
         w_down[0],
         grid=(steps,),
-        in_specs=[table, fixed(slots, cols + COUNT_LANES), pl.BlockSpec((TILE, cols), lambda i: (i, 0))],
+        in_specs=[fixed(slots, cols + COUNT_LANES), pl.BlockSpec((TILE, cols), lambda i: (i, 0))],
         out_specs=[tiles(n_blk, chunk, TILE), fixed(8, COUNT_LANES)],
-        scratch_shapes=[pltpu.VMEM((slots, cols), BF16)],
         limit=LARGE,
         flops=2 * slots * cols * ff,
         traffic=4_000_000,
     )
-    *packs, gate_pre, up_pre = call(
+    pack, gate_pre, up_pre = call(
         activate,
-        [((2,) + part, BF16)] * n_blk + [(part, F32)] * 2,
+        [((n_blk, 2 * chunk, ff), BF16), (part, F32), (part, F32)],
         near,
         got_far,
         *got_nears,
@@ -333,19 +337,23 @@
         got_up,
         parts,
     )
-    got = {d: move(packs[d], d) for d in order}
-    got = [packs[0]] + [got[d] for d in range(1, n_blk)]
-    d_gate, d_up = call(back_act, [(part, BF16)] * 2, gate_pre, up_pre, *got)
+    got = lax.all_to_all(pack, "blk", split_axis=0, concat_axis=0, tiled=True)
+    (d_gate, d_up) = call(
+        back_act,
+        [(part, BF16)] * 2,
+        gate_pre,
+        up_pre,
+        got,
+        in_specs=[fixed(*part), fixed(*part), pl.BlockSpec((n_blk, chunk, ff), lambda i: (0, 1, 0))],
+    )
     got_dg = move(d_gate, N_Y)
     got_du = [move(d_up, dy) for dy in range(1, N_Y)]
-    got, got_dg = lax.optimization_barrier((got, got_dg))
     expert_out, hidden = call(
         expert,
         [((slots, cols), BF16), ((slots, ff), BF16)],
-        comes_from,
         w_down[0],
-        *got,
-        ordered=True,
+        got,
+        in_specs=[fixed(ff, cols), fixed(n_blk, chunk, ff)],
         limit=LARGE,
         flops=2 * slots * cols * ff,
         traffic=4_000_000,
@@ -368,7 +376,7 @@
         traffic=4_000_000,
     )
     (layer_out,) = call(combine, [((rows, cols), BF16)], gate_hi, gate_lo, returned)
-    dg, du, grad_down, layer_out = lax.optimization_barrier((dg, du, grad_down, layer_out))
+    dg, du, grad_down, layer_out, turned = lax.optimization_barrier((dg, du, grad_down, layer_out, turned))
     grad_gate, grad_up = call(
         grad_tile,
         [((cols, ff), BF16)] * 2,

time: 177 us -> 164 us (0.927)
  blocking collectives: 0 us -> 26.6 us
  waiting for transfers between devices: 71.8 us -> 52.2 us
  starting transfers between devices: 62.5 us -> 48.3 us
  Pallas kernels: 35.5 us -> 30.3 us
    all_to_all x0 -> x1, blocking collectives: none -> 26.6 us  [body(): got = lax.all_to_all(pack, 'blk', split_axis=0, concat_axis=0, tiled=True)]
    ppermute x23 -> x16, waiting for transfers between devices: 45.8 us -> 25.3 us  [move(): return lax.ppermute(array, 'blk', pairs)]
    ppermute x23 -> x16, starting transfers between devices: 22.4 us -> 14 us  [move(): return lax.ppermute(array, 'blk', pairs)]
    all_to_all x3, starting transfers between devices: 40.1 us -> 34.2 us  [to_experts(): lax.all_to_all(rows.reshape(experts, CAP, cols), 'expert', split_axis=0,...]
    pallas_call x13, Pallas kernels: 35.5 us -> 30.3 us  [call(): pl.pallas_call(kernel, out_shape=outs, compiler_params=pltpu.CompilerPara...]
  transfers between devices with their start and end apart: 26 -> 19, of which waited for: 16 -> 10; matrix products, arithmetic and copies ran while one was open for 1% -> 1% of each run, Pallas kernels for 13% -> 12%
where the time goes in v2:
time: 164 us
  waiting for transfers between devices  52.2 us (32%)
  starting transfers between devices  48.3 us (29%)
  Pallas kernels  30.3 us (18%)
  blocking collectives  26.6 us (16%)
  local copies, waits for them, and re-layouts  5.18 us (3%)
    all_to_all x3, starting transfers between devices, to_experts(): lax.all_to_all(rows.reshape(experts, CAP, cols), 'expert', split_axis=0,...  34.2 us
    pallas_call x13, Pallas kernels, call(): pl.pallas_call(kernel, out_shape=outs, compiler_params=pltpu.CompilerPara...  30.3 us
    all_to_all x3, waiting for transfers between devices, to_experts(): lax.all_to_all(rows.reshape(experts, CAP, cols), 'expert', split_axis=0,...  27 us
    all_to_all x1, blocking collectives, body(): got = lax.all_to_all(pack, 'blk', split_axis=0, concat_axis=0, tiled=True)  26.6 us
    ppermute x16, waiting for transfers between devices, move(): return lax.ppermute(array, 'blk', pairs)  25.3 us
    ppermute x16, starting transfers between devices, move(): return lax.ppermute(array, 'blk', pairs)  14 us
  transfers between devices with their start and end apart: 19, of which 10 were waited for; matrix products, arithmetic and copies ran while one was open for 1% of the time, Pallas kernels for 12%

profile of v2, /device:TPU:1, one launch (start us, length us, event | category | flops | bytes accessed | tf_op | source)
XLA Modules:
  0.0 163.6 jit_solution(2169753122981773204)
XLA Ops:
  0.6 2.7 %route.1 = bf16[512,896]{1,0:T(8,128)(2,1)} custom-call(s32[8,256]{1,0:T(8,128)} %bitcast.45, bf16[256,896]{1,0:T(8,128)(2,1)} %tok_ref.1), custom_call_target="tpu_custom_call" | custom-call | tf_op jit(solution)/shard_map/route/pallas_call | solution.py:56
  3.3 12.6 %all-to-all-start = ((bf16[32,16,896]{2,1,0:T(8,128)(2,1)}), bf16[32,16,896]{2,1,0:T(8,128)(2,1)S(1)}, u32[]{:S(2)}, u32[]{:S(2)}) async-start(bf16[32,16,896]{2,1,0:T(8,128)(2,1)} %bitcast.35), calls=%async_computation | async-start | bytes 1835008 | tf_op jit(solution)/shard_map/all_to_all | solution.py:246
  16.7 3.2 %route_back.1 = (bf16[512,1024]{1,0:T(8,128)(2,1)}, bf16[256,512]{1,0:T(8,128)(2,1)}, bf16[256,512]{1,0:T(8,128)(2,1)}) custom-call(s32[8,256]{1,0:T(8,128)} %bitcast.46, s32[8,256]{1,0:T(8,128)} %bitcast.47, bf16[256,896]{1,0:T(8,128)(2,1)} %cot_ref.1), custom_call_target="tpu_custom_call" | custom-call | tf_op jit(solution)/shard_map/route_back/pallas_call | solution.py:56
  19.9 21.1 %all-to-all-done = bf16[32,16,896]{2,1,0:T(8,128)(2,1)S(1)} async-done(((bf16[32,16,896]{2,1,0:T(8,128)(2,1)}), bf16[32,16,896]{2,1,0:T(8,128)(2,1)S(1)}, u32[]{:S(2)}, u32[]{:S(2)}) %all-to-all-start) | async-done | bytes 917536 | tf_op jit(solution)/shard_map/all_to_all | solution.py:246
  40.9 6.8 %all-to-all-start.1 = ((bf16[32,16,1024]{2,1,0:T(8,128)(2,1)}), bf16[32,16,1024]{2,1,0:T(8,128)(2,1)}, u32[]{:S(2)}, u32[]{:S(2)}) async-start(bf16[32,16,1024]{2,1,0:T(8,128)(2,1)} %bitcast.39), calls=%async_computation.1 | async-start | bytes 2097152 | tf_op jit(solution)/shard_map/all_to_all | solution.py:246
  47.8 5.2 %project.1 = (bf16[4,64,768]{2,1,0:T(8,128)(2,1)}, bf16[4,64,768]{2,1,0:T(8,128)(2,1)}, bf16[2,64,1280]{2,1,0:T(8,128)(2,1)}, bf16[2,64,1280]{2,1,0:T(8,128)(2,1...) custom-call(s32[8]{0:T(128)} %stack.70.order_ref, bf16[512,896]{1,0:T(8,128)(2,1)} %bitcast.30, ...), custom_call_target="tpu_custom_call" | custom-call | flops 1879048192 | bytes 7000000 | tf_op jit(solution)/shard_map/project/pallas_call | solution.py:56
  53.0 1.3 collective-permute-start.4
  54.4 2.6 %collective-permute-start.5 = (bf16[2,64,1280]{2,1,0:T(8,128)(2,1)}, bf16[2,64,1280]{2,1,0:T(8,128)(2,1)S(1)}, u32[]{:S(2)}, u32[]{:S(2)}) collective-permute-start(bf16[2,64,1280]{2,1,0:T(8,128)(2,1)} %get-tuple-element.49), channel_id=1, source_target_pairs={{0,2},{1,3},{2,0},{3,1},{4,6},{5,7},{6,4},{7,5},{8,10},{9,11},{10,... | collective-permute-start | bytes 983048 | tf_op jit(solution)/shard_map/ppermute | solution.py:241
  58.4 5.2 %collective-permute-done.4.refs_1_.w1 = bf16[2,64,1280]{2,1,0:T(8,128)(2,1)S(1)} collective-permute-done((bf16[2,64,1280]{2,1,0:T(8,128)(2,1)}, bf16[2,64,1280]{2,1,0:T(8,128)(2,1)S(1)}, u32[]{:S(2)}, u32[]{:S(2)}) %collective-permute-start.4) | collective-permute-done | bytes 327712 | tf_op jit(solution)/shard_map/ppermute | solution.py:241
  63.6 8.1 %collective-permute-done.5.refs_2_.w2 = bf16[2,64,1280]{2,1,0:T(8,128)(2,1)S(1)} collective-permute-done((bf16[2,64,1280]{2,1,0:T(8,128)(2,1)}, bf16[2,64,1280]{2,1,0:T(8,128)(2,1)S(1)}, u32[]{:S(2)}, u32[]{:S(2)}) %collective-permute-start.5) | collective-permute-done | bytes 327712 | tf_op jit(solution)/shard_map/ppermute | solution.py:241
  75.3 1.3 collective-permute-start.1
  76.6 1.5 collective-permute-start.2
  79.1 3.9 %back.1 = (bf16[8,64,1024]{2,1,0:T(8,128)(2,1)}, s32[8,128]{1,0:T(8,128)}) custom-call(bf16[512,1024]{1,0:T(8,128)(2,1)} %bitcast.15.c_ref, bf16[1024,896]{1,0:T(8,128)(2,1)} %bitcast.36), custom_call_target="tpu_custom_call" | custom-call | flops 939524096 | bytes 4000000 | tf_op jit(solution)/shard_map/back/pallas_call | solution.py:56
  84.7 26.6 %all_to_all.20.part_ref.got_ref = bf16[8,128,1024]{2,1,0:T(8,128)(2,1)} all-to-all(bf16[8,128,1024]{2,1,0:T(8,128)(2,1)S(1)} %get-tuple-element.55), channel_id=1, replica_groups=mesh['expert'=32,'blk'=8] {'blk'}, dimensions={0} | all-to-all | bytes 4194304 | tf_op jit(solution)/shard_map/all_to_all | solution.py:340
  111.3 4.1 %expert.1 = (bf16[512,896]{1,0:T(8,128)(2,1)}, bf16[512,1024]{1,0:T(8,128)(2,1)}) custom-call(bf16[1024,896]{1,0:T(8,128)(2,1)} %bitcast.37, bf16[8,128,1024]{2,1,0:T(8,128)(2,1)} %all_to_all.20.part_ref.got_ref), custom_call_target="tpu_custom_call" | custom-call | flops 939524096 | bytes 4000000 | tf_op jit(solution)/shard_map/expert/pallas_call | solution.py:56
  115.4 14.8 %all-to-all-start.3 = ((bf16[32,16,896]{2,1,0:T(8,128)(2,1)}), bf16[32,16,896]{2,1,0:T(8,128)(2,1)S(1)}, u32[]{:S(2)}, u32[]{:S(2)}) async-start(bf16[32,16,896]{2,1,0:T(8,128)(2,1)} %bitcast.40), calls=%async_computation.3 | async-start | bytes 1835008 | tf_op jit(solution)/shard_map/all_to_all | solution.py:246
  132.6 3.0 %collective-permute-done.14 = bf16[64,1024]{1,0:T(8,128)(2,1)S(1)} collective-permute-done((bf16[64,1024]{1,0:T(8,128)(2,1)S(1)}, bf16[64,1024]{1,0:T(8,128)(2,1)S(1)}, u32[]{:S(2)}, u32[]{:S(2)}) %collective-permute-start.14) | collective-permute-done | bytes 131104 | tf_op jit(solution)/shard_map/ppermute | solution.py:241
  135.6 1.7 %collective-permute-done.13 = bf16[64,1024]{1,0:T(8,128)(2,1)S(1)} collective-permute-done((bf16[64,1024]{1,0:T(8,128)(2,1)S(1)}, bf16[64,1024]{1,0:T(8,128)(2,1)S(1)}, u32[]{:S(2)}, u32[]{:S(2)}) %collective-permute-start.13) | collective-permute-done | bytes 131104 | tf_op jit(solution)/shard_map/ppermute | solution.py:241
  137.3 3.6 %collective-permute-done.12 = bf16[64,1024]{1,0:T(8,128)(2,1)S(1)} collective-permute-done((bf16[64,1024]{1,0:T(8,128)(2,1)S(1)}, bf16[64,1024]{1,0:T(8,128)(2,1)S(1)}, u32[]{:S(2)}, u32[]{:S(2)}) %collective-permute-start.12) | collective-permute-done | bytes 131104 | tf_op jit(solution)/shard_map/ppermute | solution.py:241
  145.6 3.9 %grad_down_tile.1 = bf16[1024,896]{1,0:T(8,128)(2,1)} custom-call(bf16[512,1024]{1,0:T(8,128)(2,1)} %get-tuple-element.58.hidden_ref, bf16[512,1024]{1,0:T(8,128)(2,1)} %bitcast.15.c_ref), custom_call_target="tpu_custom_call" | custom-call | flops 939524096 | bytes 4000000 | tf_op jit(solution)/shard_map/grad_down_tile/pallas_call | solution.py:56
  149.4 5.9 %all-to-all-done.3 = bf16[32,16,896]{2,1,0:T(8,128)(2,1)S(1)} async-done(((bf16[32,16,896]{2,1,0:T(8,128)(2,1)}), bf16[32,16,896]{2,1,0:T(8,128)(2,1)S(1)}, u32[]{:S(2)}, u32[]{:S(2)}) %all-to-all-start.3) | async-done | bytes 917536 | tf_op jit(solution)/shard_map/all_to_all | solution.py:246
  155.3 1.5 combine.1
  157.8 1.5 collective-permute-done.15.u1
  159.3 4.3 %grad_tile.1 = (bf16[896,1024]{1,0:T(8,128)(2,1)}, bf16[896,1024]{1,0:T(8,128)(2,1)}) custom-call(bf16[896,512]{1,0:T(8,128)(2,1)S(1)} %turn.1.x_ref, bf16[2,64,1024]{2,1,0:T(8,128)(2,1)S(1)} %pad_maximum_fusion.1.g0, bf16[2,64,1024]{2,1,0:T(8,128)(2,1)} %collective-permute-done.9.g1, bf16[2,64,1024]{2,1,0:T(8,128)(2,1)} %collective-permute-done.10.g2, ...), custom_call_target="tpu_custom_call" | custom-call | flops 1879048192 | bytes 6000000 | tf_op jit(solution)/shard_map/grad_tile/pallas_call | solution.py:56
  (53 shorter events, 16.1 us)
Async XLA Ops:
  3.3 37.6 %all-to-all-start = ((bf16[32,16,896]{2,1,0:T(8,128)(2,1)}), bf16[32,16,896]{2,1,0:T(8,128)(2,1)S(1)}, u32[]{:S(2)}, u32[]{:S(2)}) async-start(bf16[32,16,896]{2,1,0:T(8,128)(2,1)} %bitcast.35), calls=%async_computation | async-start | bytes 1835008 | tf_op jit(solution)/shard_map/all_to_all | solution.py:246
  40.9 38.2 %all-to-all-start.1 = ((bf16[32,16,1024]{2,1,0:T(8,128)(2,1)}), bf16[32,16,1024]{2,1,0:T(8,128)(2,1)}, u32[]{:S(2)}, u32[]{:S(2)}) async-start(bf16[32,16,1024]{2,1,0:T(8,128)(2,1)} %bitcast.39), calls=%async_computation.1 | async-start | bytes 2097152 | tf_op jit(solution)/shard_map/all_to_all | solution.py:246
  53.0 10.6 %collective-permute-start.4 = (bf16[2,64,1280]{2,1,0:T(8,128)(2,1)}, bf16[2,64,1280]{2,1,0:T(8,128)(2,1)S(1)}, u32[]{:S(2)}, u32[]{:S(2)}) collective-permute-start(bf16[2,64,1280]{2,1,0:T(8,128)(2,1)} %get-tuple-element.48), channel_id=1, source_target_pairs={{0,1},{1,2},{2,3},{3,0},{4,5},{5,6},{6,7},{7,4},{8,9},{9,10},{10,1... | collective-permute-start | bytes 983048 | tf_op jit(solution)/shard_map/ppermute | solution.py:241
  54.4 17.4 %collective-permute-start.5 = (bf16[2,64,1280]{2,1,0:T(8,128)(2,1)}, bf16[2,64,1280]{2,1,0:T(8,128)(2,1)S(1)}, u32[]{:S(2)}, u32[]{:S(2)}) collective-permute-start(bf16[2,64,1280]{2,1,0:T(8,128)(2,1)} %get-tuple-element.49), channel_id=1, source_target_pairs={{0,2},{1,3},{2,0},{3,1},{4,6},{5,7},{6,4},{7,5},{8,10},{9,11},{10,... | collective-permute-start | bytes 983048 | tf_op jit(solution)/shard_map/ppermute | solution.py:241
  57.0 17.2 %collective-permute-start = (bf16[4,64,768]{2,1,0:T(8,128)(2,1)}, bf16[4,64,768]{2,1,0:T(8,128)(2,1)S(1)}, u32[]{:S(2)}, u32[]{:S(2)}) collective-permute-start(bf16[4,64,768]{2,1,0:T(8,128)(2,1)} %get-tuple-element.43), channel_id=1, source_target_pairs={{0,4},{1,5},{2,6},{3,7},{4,0},{5,1},{6,2},{7,3},{8,12},{9,13},{10,... | collective-permute-start | bytes 1179656 | tf_op jit(solution)/shard_map/ppermute | solution.py:241
  57.3 14.4 %collective-permute-start.6 = (bf16[2,64,1280]{2,1,0:T(8,128)(2,1)}, bf16[2,64,1280]{2,1,0:T(8,128)(2,1)S(1)}, u32[]{:S(2)}, u32[]{:S(2)}) collective-permute-start(bf16[2,64,1280]{2,1,0:T(8,128)(2,1)} %get-tuple-element.50), channel_id=1, source_target_pairs={{0,3},{1,0},{2,1},{3,2},{4,7},{5,4},{6,5},{7,6},{8,11},{9,8},{10,9... | collective-permute-start | bytes 983048 | tf_op jit(solution)/shard_map/ppermute | solution.py:241
  72.8 10.3 %collective-permute-start.7 = (bf16[64,1280]{1,0:T(8,128)(2,1)S(1)}, bf16[64,1280]{1,0:T(8,128)(2,1)S(1)}, u32[]{:S(2)}, u32[]{:S(2)}) collective-permute-start(bf16[64,1280]{1,0:T(8,128)(2,1)S(1)} %meet_far.1), channel_id=1, source_target_pairs={{0,4},{1,5},{2,6},{3,7},{4,0},{5,1},{6,2},{7,3},{8,12},{9,13},{10,... | collective-permute-start | bytes 491528 | tf_op jit(solution)/shard_map/ppermute | solution.py:241
  75.3 7.8 %copy-start.4 = (bf16[4,64,768]{2,1,0:T(8,128)(2,1)S(1)}, bf16[4,64,768]{2,1,0:T(8,128)(2,1)}, u32[]{:S(2)}) copy-start(bf16[4,64,768]{2,1,0:T(8,128)(2,1)} %get-tuple-element.42.near_ref) | copy-start | bytes 1179652
  75.3 7.8 %collective-permute-start.1 = (bf16[64,768]{1,0:T(8,128)(2,1)S(1)}, bf16[64,768]{1,0:T(8,128)(2,1)S(1)}, u32[]{:S(2)}, u32[]{:S(2)}) collective-permute-start(bf16[64,768]{1,0:T(8,128)(2,1)S(1)} %get-tuple-element.44), channel_id=1, source_target_pairs={{0,1},{1,2},{2,3},{3,0},{4,5},{5,6},{6,7},{7,4},{8,9},{9,10},{10,1... | collective-permute-start | bytes 294920 | tf_op jit(solution)/shard_map/ppermute | solution.py:241
  76.6 6.4 %collective-permute-start.2 = (bf16[64,768]{1,0:T(8,128)(2,1)S(1)}, bf16[64,768]{1,0:T(8,128)(2,1)S(1)}, u32[]{:S(2)}, u32[]{:S(2)}) collective-permute-start(bf16[64,768]{1,0:T(8,128)(2,1)S(1)} %get-tuple-element.45), channel_id=1, source_target_pairs={{0,2},{1,3},{2,0},{3,1},{4,6},{5,7},{6,4},{7,5},{8,10},{9,11},{10,... | collective-permute-start | bytes 294920 | tf_op jit(solution)/shard_map/ppermute | solution.py:241
  78.2 4.9 %collective-permute-start.3 = (bf16[64,768]{1,0:T(8,128)(2,1)S(1)}, bf16[64,768]{1,0:T(8,128)(2,1)S(1)}, u32[]{:S(2)}, u32[]{:S(2)}) collective-permute-start(bf16[64,768]{1,0:T(8,128)(2,1)S(1)} %get-tuple-element.46), channel_id=1, source_target_pairs={{0,3},{1,0},{2,1},{3,2},{4,7},{5,4},{6,5},{7,6},{8,11},{9,8},{10,9... | collective-permute-start | bytes 294920 | tf_op jit(solution)/shard_map/ppermute | solution.py:241
  111.3 18.9 %copy-start = (bf16[8,128,1024]{2,1,0:T(8,128)(2,1)S(1)}, bf16[8,128,1024]{2,1,0:T(8,128)(2,1)}, u32[]{:S(2)}) copy-start(bf16[8,128,1024]{2,1,0:T(8,128)(2,1)} %all_to_all.20.part_ref.got_ref) | copy-start | bytes 6291460
  115.4 39.9 %all-to-all-start.3 = ((bf16[32,16,896]{2,1,0:T(8,128)(2,1)}), bf16[32,16,896]{2,1,0:T(8,128)(2,1)S(1)}, u32[]{:S(2)}, u32[]{:S(2)}) async-start(bf16[32,16,896]{2,1,0:T(8,128)(2,1)} %bitcast.40), calls=%async_computation.3 | async-start | bytes 1835008 | tf_op jit(solution)/shard_map/all_to_all | solution.py:246
  130.2 11.0 %copy-start.2 = (bf16[32,16,896]{2,1,0:T(8,128)(2,1)S(1)}, bf16[32,16,896]{2,1,0:T(8,128)(2,1)}, u32[]{:S(2)}) copy-start(bf16[32,16,896]{2,1,0:T(8,128)(2,1)} %copy-done.1) | copy-start | bytes 2752516
  130.5 5.1 %collective-permute-start.14 = (bf16[64,1024]{1,0:T(8,128)(2,1)S(1)}, bf16[64,1024]{1,0:T(8,128)(2,1)S(1)}, u32[]{:S(2)}, u32[]{:S(2)}) collective-permute-start(bf16[64,1024]{1,0:T(8,128)(2,1)S(1)} %get-tuple-element.57), channel_id=1, source_target_pairs={{0,3},{1,0},{2,1},{3,2},{4,7},{5,4},{6,5},{7,6},{8,11},{9,8},{10,9... | collective-permute-start | bytes 393224 | tf_op jit(solution)/shard_map/ppermute | solution.py:241
  131.3 6.1 %collective-permute-start.13 = (bf16[64,1024]{1,0:T(8,128)(2,1)S(1)}, bf16[64,1024]{1,0:T(8,128)(2,1)S(1)}, u32[]{:S(2)}, u32[]{:S(2)}) collective-permute-start(bf16[64,1024]{1,0:T(8,128)(2,1)S(1)} %get-tuple-element.57), channel_id=1, source_target_pairs={{0,2},{1,3},{2,0},{3,1},{4,6},{5,7},{6,4},{7,5},{8,10},{9,11},{10,... | collective-permute-start | bytes 393224 | tf_op jit(solution)/shard_map/ppermute | solution.py:241
  132.5 8.5 %collective-permute-start.12 = (bf16[64,1024]{1,0:T(8,128)(2,1)S(1)}, bf16[64,1024]{1,0:T(8,128)(2,1)S(1)}, u32[]{:S(2)}, u32[]{:S(2)}) collective-permute-start(bf16[64,1024]{1,0:T(8,128)(2,1)S(1)} %get-tuple-element.57), channel_id=1, source_target_pairs={{0,1},{1,2},{2,3},{3,0},{4,5},{5,6},{6,7},{7,4},{8,9},{9,10},{10,1... | collective-permute-start | bytes 393224 | tf_op jit(solution)/shard_map/ppermute | solution.py:241
  132.5 9.6 %collective-permute-start.8 = (bf16[64,1024]{1,0:T(8,128)(2,1)S(1)}, bf16[64,1024]{1,0:T(8,128)(2,1)S(1)}, u32[]{:S(2)}, u32[]{:S(2)}) collective-permute-start(bf16[64,1024]{1,0:T(8,128)(2,1)S(1)} %get-tuple-element.56), channel_id=1, source_target_pairs={{0,4},{1,5},{2,6},{3,7},{4,0},{5,1},{6,2},{7,3},{8,12},{9,13},{10,... | collective-permute-start | bytes 393224 | tf_op jit(solution)/shard_map/ppermute | solution.py:241
  141.0 18.2 %collective-permute-start.15 = (bf16[4,64,1024]{2,1,0:T(8,128)(2,1)S(1)}, bf16[4,64,1024]{2,1,0:T(8,128)(2,1)}, u32[]{:S(2)}, u32[]{:S(2)}) collective-permute-start(bf16[4,64,1024]{2,1,0:T(8,128)(2,1)S(1)} %pad_maximum_fusion.u0), channel_id=1, source_target_pairs={{0,4},{1,5},{2,6},{3,7},{4,0},{5,1},{6,2},{7,3},{8,12},{9,13},{10,... | collective-permute-start | bytes 1572872 | tf_op jit(solution)/shard_map/ppermute | solution.py:241
  142.1 14.7 %collective-permute-start.11 = (bf16[2,64,1024]{2,1,0:T(8,128)(2,1)S(1)}, bf16[2,64,1024]{2,1,0:T(8,128)(2,1)S(1)}, u32[]{:S(2)}, u32[]{:S(2)}) collective-permute-start(bf16[2,64,1024]{2,1,0:T(8,128)(2,1)S(1)} %pad_maximum_fusion.1.g0), channel_id=1, source_target_pairs={{0,3},{1,0},{2,1},{3,2},{4,7},{5,4},{6,5},{7,6},{8,11},{9,8},{10,9... | collective-permute-start | bytes 786440 | tf_op jit(solution)/shard_map/ppermute | solution.py:241
  142.2 14.6 %collective-permute-start.10 = (bf16[2,64,1024]{2,1,0:T(8,128)(2,1)S(1)}, bf16[2,64,1024]{2,1,0:T(8,128)(2,1)}, u32[]{:S(2)}, u32[]{:S(2)}) collective-permute-start(bf16[2,64,1024]{2,1,0:T(8,128)(2,1)S(1)} %pad_maximum_fusion.1.g0), channel_id=1, source_target_pairs={{0,2},{1,3},{2,0},{3,1},{4,6},{5,7},{6,4},{7,5},{8,10},{9,11},{10,... | collective-permute-start | bytes 786440 | tf_op jit(solution)/shard_map/ppermute | solution.py:241
  143.6 14.2 %collective-permute-start.9 = (bf16[2,64,1024]{2,1,0:T(8,128)(2,1)S(1)}, bf16[2,64,1024]{2,1,0:T(8,128)(2,1)}, u32[]{:S(2)}, u32[]{:S(2)}) collective-permute-start(bf16[2,64,1024]{2,1,0:T(8,128)(2,1)S(1)} %pad_maximum_fusion.1.g0), channel_id=1, source_target_pairs={{0,1},{1,2},{2,3},{3,0},{4,5},{5,6},{6,7},{7,4},{8,9},{9,10},{10,1... | collective-permute-start | bytes 786440 | tf_op jit(solution)/shard_map/ppermute | solution.py:241
  145.6 9.7 %copy-start.8 = (bf16[256,512]{1,0:T(8,128)(2,1)S(1)}, bf16[256,512]{1,0:T(8,128)(2,1)}, u32[]{:S(2)}) copy-start(bf16[256,512]{1,0:T(8,128)(2,1)} %get-tuple-element.59.hi_ref) | copy-start | bytes 786436
  145.6 9.7 %copy-start.9 = (bf16[256,512]{1,0:T(8,128)(2,1)S(1)}, bf16[256,512]{1,0:T(8,128)(2,1)}, u32[]{:S(2)}) copy-start(bf16[256,512]{1,0:T(8,128)(2,1)} %get-tuple-element.60.lo_ref) | copy-start | bytes 786436
  (5 other events, 17.9 us)

commit v3 on v2

--- a/solution.py
+++ b/solution.py
@@ -157,7 +157,7 @@
     out[...] = sum(r[1].astype(F32) for r in refs[:-1]).astype(BF16)
 
 
-def activate(near_ref, got_ref, n1, n2, n3, w0, w1, w2, w3, got_w, part_ref, pack_ref, gate_ref, up_ref):
+def activate(near_ref, got_ref, n1, n2, n3, w0, w1, w2, w3, got_w, pack_ref, gate_ref, up_ref):
     near = near_ref[0].astype(F32) + got_ref[0].astype(F32)
     for r in (n1, n2, n3):
         near = near + r[...].astype(F32)
@@ -171,19 +171,20 @@
         up_ref[:, i * TILE : (i + 1) * TILE] = wide[:, i * span + TILE - NEAR : (i + 1) * span]
     gate = gate_ref[...]
     hidden = (gate * jax.nn.sigmoid(gate) * up_ref[...]).astype(BF16)
-    chunk = hidden.shape[0]
     for d in range(pack_ref.shape[0]):
-        pack_ref[d, :chunk] = hidden
-        pack_ref[d, chunk:] = part_ref[d]
-
-
-def back(c_ref, w_ref, part_ref, load_ref):
-    slots = c_ref.shape[0]
-    cols = w_ref.shape[1]
-    chunk = part_ref.shape[1]
-    partial = dot(c_ref[:, :cols], w_ref[...], ((1,), (1,))).astype(BF16)
-    for d in range(part_ref.shape[0]):
-        part_ref[d] = partial[d * chunk : (d + 1) * chunk]
+        pack_ref[d] = hidden
+
+
+def back(order_ref, c_ref, w_ref, *rest):
+    outs, (load_ref, held) = rest[:-2], rest[-2:]
+    slots, cols = held.shape
+    chunk = outs[0].shape[1]
+    in_order(order_ref, c_ref, held)
+    partial = dot(held[...], w_ref[...], ((1,), (1,))).astype(BF16)
+    for dx in range(2):
+        for dy, out in enumerate(outs):
+            at = (dx * N_Y + dy) * chunk
+            out[dx] = partial[at : at + chunk]
 
     @pl.when(pl.program_id(0) == 0)
     def _():
@@ -191,17 +192,14 @@
         load_ref[...] = matmul(counted, c_ref[:, cols:]).astype(jnp.int32)
 
 
-def expert(w_ref, got_ref, out_ref, hidden_ref):
-    n, chunk = got_ref.shape[0], got_ref.shape[1]
-    for d in range(n):
-        hidden_ref[d * chunk : (d + 1) * chunk, :] = got_ref[d]
+def expert(w_ref, hidden_ref, out_ref):
     out_ref[...] = matmul(hidden_ref[...], w_ref[...]).astype(BF16)
 
 
-def back_act(gate_ref, up_ref, part_ref, dg_ref, du_ref):
-    d = part_ref[0].astype(F32)
-    for i in range(1, part_ref.shape[0]):
-        d = d + part_ref[i].astype(F32)
+def back_act(gate_ref, up_ref, p0, p1, p2, p3, got, dg_ref, du_ref):
+    d = got[...].astype(F32)
+    for r in (p0, p1, p2, p3):
+        d = d + r[0].astype(F32)
     gate = gate_ref[...]
     sigma = jax.nn.sigmoid(gate)
     dg_ref[...] = (d * up_ref[...] * sigma * (1.0 + gate * (1.0 - sigma))).astype(BF16)
@@ -303,62 +301,50 @@
 
     got_far = move(far, N_Y)
     got_ups = [ups[0]] + [move(ups[dy], dy) for dy in range(1, N_Y)]
-    (turned,) = call(
-        turn,
-        [((cols, slots), BF16)],
-        comes_from,
-        arrived,
-        ordered=True,
-        scratch_shapes=[pltpu.VMEM((slots, cols), BF16)],
-    )
     nears = call(meet_near, [((chunk, NEAR * steps), BF16)] * (N_Y - 1), near, got_far)
     (up_far,) = call(meet_far, [((chunk, span * steps), BF16)], *got_ups)
     got_nears = [move(g, dy) for dy, g in enumerate(nears, 1)]
     got_up = move(up_far, N_Y)
-    parts, loads = call(
+    *parts, loads = call(
         back,
-        [((n_blk,) + part, BF16), ((8, COUNT_LANES), jnp.int32)],
+        [((2,) + part, BF16)] * N_Y + [((8, COUNT_LANES), jnp.int32)],
+        goes_to,
         arrived_cot,
         w_down[0],
         grid=(steps,),
-        in_specs=[fixed(slots, cols + COUNT_LANES), pl.BlockSpec((TILE, cols), lambda i: (i, 0))],
-        out_specs=[tiles(n_blk, chunk, TILE), fixed(8, COUNT_LANES)],
+        in_specs=[table, fixed(slots, cols + COUNT_LANES), pl.BlockSpec((TILE, cols), lambda i: (i, 0))],
+        out_specs=[tiles(2, chunk, TILE)] * N_Y + [fixed(8, COUNT_LANES)],
+        scratch_shapes=[pltpu.VMEM((slots, cols), BF16)],
         limit=LARGE,
         flops=2 * slots * cols * ff,
         traffic=4_000_000,
     )
-    pack, gate_pre, up_pre = call(
+    hidden, gate_pre, up_pre = call(
         activate,
-        [((n_blk, 2 * chunk, ff), BF16), (part, F32), (part, F32)],
+        [((n_blk,) + part, BF16), (part, F32), (part, F32)],
         near,
         got_far,
         *got_nears,
         *got_ups,
         got_up,
-        parts,
-    )
-    got = lax.all_to_all(pack, "blk", split_axis=0, concat_axis=0, tiled=True)
-    (d_gate, d_up) = call(
-        back_act,
-        [(part, BF16)] * 2,
-        gate_pre,
-        up_pre,
-        got,
-        in_specs=[fixed(*part), fixed(*part), pl.BlockSpec((n_blk, chunk, ff), lambda i: (0, 1, 0))],
-    )
-    got_dg = move(d_gate, N_Y)
-    got_du = [move(d_up, dy) for dy in range(1, N_Y)]
-    expert_out, hidden = call(
+    )
+    hidden = lax.all_to_all(hidden, "blk", split_axis=0, concat_axis=0, tiled=True).reshape(slots, ff)
+    got = [parts[0]] + [move(parts[dy], dy) for dy in range(1, N_Y)]
+    (expert_out,) = call(
         expert,
-        [((slots, cols), BF16), ((slots, ff), BF16)],
+        [((slots, cols), BF16)],
         w_down[0],
-        got,
-        in_specs=[fixed(ff, cols), fixed(n_blk, chunk, ff)],
+        hidden,
         limit=LARGE,
         flops=2 * slots * cols * ff,
         traffic=4_000_000,
     )
     returned = to_experts(expert_out, experts)
+    (d_far,) = call(meet_far, [(part, BF16)], *got, flops=10**11)
+    got_d = move(d_far, N_Y)
+    d_gate, d_up = call(back_act, [(part, BF16)] * 2, gate_pre, up_pre, *got, got_d)
+    got_dg = move(d_gate, N_Y)
+    got_du = [move(d_up, dy) for dy in range(1, N_Y)]
     dg_pair = jnp.stack([d_gate, got_dg])
     du_four = jnp.stack([d_up] + got_du)
     dg = [dg_pair] + [move(dg_pair, dy) for dy in range(1, N_Y)]
@@ -374,6 +360,15 @@
         limit=LARGE,
         flops=2 * slots * cols * ff,
         traffic=4_000_000,
+    )
+    arrived, grad_down = lax.optimization_barrier((arrived, grad_down))
+    (turned,) = call(
+        turn,
+        [((cols, slots), BF16)],
+        comes_from,
+        arrived,
+        ordered=True,
+        scratch_shapes=[pltpu.VMEM((slots, cols), BF16)],
     )
     (layer_out,) = call(combine, [((rows, cols), BF16)], gate_hi, gate_lo, returned)
     dg, du, grad_down, layer_out, turned = lax.optimization_barrier((dg, du, grad_down, layer_out, turned))

time: 164 us -> 161 us (0.982)
  blocking collectives: 26.6 us -> 0 us
  starting transfers between devices: 48.3 us -> 63.7 us
  waiting for transfers between devices: 52.2 us -> 59.6 us
    all_to_all x1 -> x0, blocking collectives: 26.6 us -> none  [body(): got = lax.all_to_all(pack, 'blk', split_axis=0, concat_axis=0, tiled=True)]
    ppermute x16 -> x20, starting transfers between devices: 14 us -> 25.6 us  [move(): return lax.ppermute(array, 'blk', pairs)]
    ppermute x16 -> x20, waiting for transfers between devices: 25.3 us -> 35.9 us  [move(): return lax.ppermute(array, 'blk', pairs)]
    all_to_all x3, waiting for transfers between devices: 27 us -> 21.1 us  [to_experts(): lax.all_to_all(rows.reshape(experts, CAP, cols), 'expert', split_axis=0,...]
    all_to_all x0 -> x1, starting transfers between devices: none -> 4.24 us  [body(): lax.all_to_all(hidden, 'blk', split_axis=0, concat_axis=0, tiled=True)]
    all_to_all x0 -> x1, waiting for transfers between devices: none -> 2.65 us  [body(): lax.all_to_all(hidden, 'blk', split_axis=0, concat_axis=0, tiled=True)]
    pallas_call x13 -> x14, Pallas kernels: 30.3 us -> 31.3 us  [call(): pl.pallas_call(kernel, out_shape=outs, compiler_params=pltpu.CompilerPara...]
  transfers between devices with their start and end apart: 19 -> 24, of which waited for: 10 -> 12; matrix products, arithmetic and copies ran while one was open for 1% -> 1% of each run, Pallas kernels for 12% -> 15%
where the time goes in v3:
time: 161 us; the launch traced here: 160 us
  starting transfers between devices  63.7 us (40%)
  waiting for transfers between devices  59.6 us (37%)
  Pallas kernels  31.3 us (19%)
  local copies, waits for them, and re-layouts  4.15 us (3%)
    ppermute x20, waiting for transfers between devices, move(): return lax.ppermute(array, 'blk', pairs)  35.9 us
    all_to_all x3, starting transfers between devices, to_experts(): lax.all_to_all(rows.reshape(experts, CAP, cols), 'expert', split_axis=0,...  33.8 us
    pallas_call x14, Pallas kernels, call(): pl.pallas_call(kernel, out_shape=outs, compiler_params=pltpu.CompilerPara...  31.3 us
    ppermute x20, starting transfers between devices, move(): return lax.ppermute(array, 'blk', pairs)  25.6 us
    all_to_all x3, waiting for transfers between devices, to_experts(): lax.all_to_all(rows.reshape(experts, CAP, cols), 'expert', split_axis=0,...  21.1 us
    all_to_all x1, starting transfers between devices, body(): lax.all_to_all(hidden, 'blk', split_axis=0, concat_axis=0, tiled=True)  4.24 us
  transfers between devices with their start and end apart: 24, of which 12 were waited for; matrix products, arithmetic and copies ran while one was open for 1% of the time, Pallas kernels for 15%

profile of v3, /device:TPU:1, one launch (start us, length us, event | category | flops | bytes accessed | tf_op | source)
XLA Modules:
  0.0 159.7 jit_solution(3971682234517755042)
XLA Ops:
  0.6 2.7 %route.1 = bf16[512,896]{1,0:T(8,128)(2,1)} custom-call(s32[8,256]{1,0:T(8,128)} %bitcast.48, bf16[256,896]{1,0:T(8,128)(2,1)} %tok_ref.1), custom_call_target="tpu_custom_call" | custom-call | tf_op jit(solution)/shard_map/route/pallas_call | solution.py:56
  3.3 12.6 %all-to-all-start = ((bf16[32,16,896]{2,1,0:T(8,128)(2,1)}), bf16[32,16,896]{2,1,0:T(8,128)(2,1)S(1)}, u32[]{:S(2)}, u32[]{:S(2)}) async-start(bf16[32,16,896]{2,1,0:T(8,128)(2,1)} %bitcast.38), calls=%async_computation | async-start | bytes 1835008 | tf_op jit(solution)/shard_map/all_to_all | solution.py:244
  16.7 3.2 %route_back.1 = (bf16[512,1024]{1,0:T(8,128)(2,1)}, bf16[256,512]{1,0:T(8,128)(2,1)}, bf16[256,512]{1,0:T(8,128)(2,1)}) custom-call(s32[8,256]{1,0:T(8,128)} %bitcast.49, s32[8,256]{1,0:T(8,128)} %bitcast.50, bf16[256,896]{1,0:T(8,128)(2,1)} %cot_ref.1), custom_call_target="tpu_custom_call" | custom-call | tf_op jit(solution)/shard_map/route_back/pallas_call | solution.py:56
  19.9 21.0 %all-to-all-done = bf16[32,16,896]{2,1,0:T(8,128)(2,1)S(1)} async-done(((bf16[32,16,896]{2,1,0:T(8,128)(2,1)}), bf16[32,16,896]{2,1,0:T(8,128)(2,1)S(1)}, u32[]{:S(2)}, u32[]{:S(2)}) %all-to-all-start) | async-done | bytes 917536 | tf_op jit(solution)/shard_map/all_to_all | solution.py:244
  40.9 6.2 %all-to-all-start.1 = ((bf16[32,16,1024]{2,1,0:T(8,128)(2,1)}), bf16[32,16,1024]{2,1,0:T(8,128)(2,1)S(1)}, u32[]{:S(2)}, u32[]{:S(2)}) async-start(bf16[32,16,1024]{2,1,0:T(8,128)(2,1)} %bitcast.43), calls=%async_computation.1 | async-start | bytes 2097152 | tf_op jit(solution)/shard_map/all_to_all | solution.py:244
  47.1 5.2 %project.1 = (bf16[4,64,768]{2,1,0:T(8,128)(2,1)}, bf16[4,64,768]{2,1,0:T(8,128)(2,1)}, bf16[2,64,1280]{2,1,0:T(8,128)(2,1)}, bf16[2,64,1280]{2,1,0:T(8,128)(2,1...) custom-call(s32[8]{0:T(128)} %stack.70.order_ref, bf16[512,896]{1,0:T(8,128)(2,1)} %bitcast.31, ...), custom_call_target="tpu_custom_call" | custom-call | flops 1879048192 | bytes 7000000 | tf_op jit(solution)/shard_map/project/pallas_call | solution.py:56
  53.7 2.6 %collective-permute-start.5 = (bf16[2,64,1280]{2,1,0:T(8,128)(2,1)}, bf16[2,64,1280]{2,1,0:T(8,128)(2,1)S(1)}, u32[]{:S(2)}, u32[]{:S(2)}) collective-permute-start(bf16[2,64,1280]{2,1,0:T(8,128)(2,1)} %get-tuple-element.52), channel_id=1, source_target_pairs={{0,2},{1,3},{2,0},{3,1},{4,6},{5,7},{6,4},{7,5},{8,10},{9,11},{10,... | collective-permute-start | bytes 983048 | tf_op jit(solution)/shard_map/ppermute | solution.py:239
  57.7 5.2 %collective-permute-done.4.refs_1_.w1 = bf16[2,64,1280]{2,1,0:T(8,128)(2,1)S(1)} collective-permute-done((bf16[2,64,1280]{2,1,0:T(8,128)(2,1)}, bf16[2,64,1280]{2,1,0:T(8,128)(2,1)S(1)}, u32[]{:S(2)}, u32[]{:S(2)}) %collective-permute-start.4) | collective-permute-done | bytes 327712 | tf_op jit(solution)/shard_map/ppermute | solution.py:239
  62.9 8.1 %collective-permute-done.5.refs_2_.w2 = bf16[2,64,1280]{2,1,0:T(8,128)(2,1)S(1)} collective-permute-done((bf16[2,64,1280]{2,1,0:T(8,128)(2,1)}, bf16[2,64,1280]{2,1,0:T(8,128)(2,1)S(1)}, u32[]{:S(2)}, u32[]{:S(2)}) %collective-permute-start.5) | collective-permute-done | bytes 327712 | tf_op jit(solution)/shard_map/ppermute | solution.py:239
  79.4 2.8 %collective-permute-done.2.n2 = bf16[64,768]{1,0:T(8,128)(2,1)S(1)} collective-permute-done((bf16[64,768]{1,0:T(8,128)(2,1)S(1)}, bf16[64,768]{1,0:T(8,128)(2,1)S(1)}, u32[]{:S(2)}, u32[]{:S(2)}) %collective-permute-start.2) | collective-permute-done | bytes 98336 | tf_op jit(solution)/shard_map/ppermute | solution.py:239
  83.5 4.2 %all-to-all-start.2 = ((bf16[8,64,1024]{2,1,0:T(8,128)(2,1)}), bf16[8,64,1024]{2,1,0:T(8,128)(2,1)}, u32[]{:S(2)}, u32[]{:S(2)}) async-start(bf16[8,64,1024]{2,1,0:T(8,128)(2,1)} %get-tuple-element.63), calls=%async_computation.2 | async-start | bytes 2097152 | tf_op jit(solution)/shard_map/all_to_all | solution.py:331
  87.7 4.0 %back.1 = (bf16[2,64,1024]{2,1,0:T(8,128)(2,1)}, bf16[2,64,1024]{2,1,0:T(8,128)(2,1)}, bf16[2,64,1024]{2,1,0:T(8,128)(2,1)}, bf16[2,64,1024]{2,1,0:T(8,128)(2,1)}, s32[8,128]{1,0:T(8,128)}) custom-call(s32[8]{0:T(128)} %stack.70.order_ref, bf16[512,1024]{1,0:T(8,128)(2,1)} %bitcast.36, bf16[1024,896]{1,0:T(8,128)(2,1)} %bitcast.40), custom_call_target="tpu_custom_call" | custom-call | flops 939524096 | bytes 4000000 | tf_op jit(solution)/shard_map/back/pallas_call | solution.py:56
  93.2 2.4 %collective-permute-start.9 = (bf16[2,64,1024]{2,1,0:T(8,128)(2,1)}, bf16[2,64,1024]{2,1,0:T(8,128)(2,1)S(1)}, u32[]{:S(2)}, u32[]{:S(2)}) collective-permute-start(bf16[2,64,1024]{2,1,0:T(8,128)(2,1)} %get-tuple-element.59), channel_id=1, source_target_pairs={{0,2},{1,3},{2,0},{3,1},{4,6},{5,7},{6,4},{7,5},{8,10},{9,11},{10,... | collective-permute-start | bytes 786440 | tf_op jit(solution)/shard_map/ppermute | solution.py:239
  96.7 2.6 %all-to-all-done.2 = bf16[8,64,1024]{2,1,0:T(8,128)(2,1)} async-done(((bf16[8,64,1024]{2,1,0:T(8,128)(2,1)}), bf16[8,64,1024]{2,1,0:T(8,128)(2,1)}, u32[]{:S(2)}, u32[]{:S(2)}) %all-to-all-start.2) | async-done | bytes 1048608 | tf_op jit(solution)/shard_map/all_to_all | solution.py:331
  99.4 4.0 %expert.1 = bf16[512,896]{1,0:T(8,128)(2,1)} custom-call(bf16[1024,896]{1,0:T(8,128)(2,1)} %bitcast.41, bf16[512,1024]{1,0:T(8,128)(2,1)} %bitcast.23.hidden_ref), custom_call_target="tpu_custom_call" | custom-call | flops 939524096 | bytes 4000000 | tf_op jit(solution)/shard_map/expert/pallas_call | solution.py:56
  103.3 15.1 %all-to-all-start.3 = ((bf16[32,16,896]{2,1,0:T(8,128)(2,1)}), bf16[32,16,896]{2,1,0:T(8,128)(2,1)S(1)}, u32[]{:S(2)}, u32[]{:S(2)}) async-start(bf16[32,16,896]{2,1,0:T(8,128)(2,1)} %bitcast.39), calls=%async_computation.3 | async-start | bytes 1835008 | tf_op jit(solution)/shard_map/all_to_all | solution.py:244
  118.8 6.4 %collective-permute-done.11.got = bf16[64,1024]{1,0:T(8,128)(2,1)S(1)} collective-permute-done((bf16[64,1024]{1,0:T(8,128)(2,1)S(1)}, bf16[64,1024]{1,0:T(8,128)(2,1)S(1)}, u32[]{:S(2)}, u32[]{:S(2)}) %collective-permute-start.11) | collective-permute-done | bytes 131104 | tf_op jit(solution)/shard_map/ppermute | solution.py:239
  125.4 2.2 %collective-permute-start.18 = (bf16[64,1024]{1,0:T(8,128)(2,1)S(1)}, bf16[64,1024]{1,0:T(8,128)(2,1)S(1)}, u32[]{:S(2)}, u32[]{:S(2)}) collective-permute-start(bf16[64,1024]{1,0:T(8,128)(2,1)S(1)} %get-tuple-element.62), channel_id=1, source_target_pairs={{0,3},{1,0},{2,1},{3,2},{4,7},{5,4},{6,5},{7,6},{8,11},{9,8},{10,9... | collective-permute-start | bytes 393224 | tf_op jit(solution)/shard_map/ppermute | solution.py:239
  127.6 6.0 %collective-permute-start.17 = (bf16[64,1024]{1,0:T(8,128)(2,1)S(1)}, bf16[64,1024]{1,0:T(8,128)(2,1)S(1)}, u32[]{:S(2)}, u32[]{:S(2)}) collective-permute-start(bf16[64,1024]{1,0:T(8,128)(2,1)S(1)} %get-tuple-element.62), channel_id=1, source_target_pairs={{0,2},{1,3},{2,0},{3,1},{4,6},{5,7},{6,4},{7,5},{8,10},{9,11},{10,... | collective-permute-start | bytes 393224 | tf_op jit(solution)/shard_map/ppermute | solution.py:239
  136.3 3.2 %collective-permute-done.16 = bf16[64,1024]{1,0:T(8,128)(2,1)S(1)} collective-permute-done((bf16[64,1024]{1,0:T(8,128)(2,1)S(1)}, bf16[64,1024]{1,0:T(8,128)(2,1)S(1)}, u32[]{:S(2)}, u32[]{:S(2)}) %collective-permute-start.16) | collective-permute-done | bytes 131104 | tf_op jit(solution)/shard_map/ppermute | solution.py:239
  143.6 3.9 %grad_down_tile.1 = bf16[1024,896]{1,0:T(8,128)(2,1)} custom-call(bf16[512,1024]{1,0:T(8,128)(2,1)} %bitcast.23.hidden_ref, bf16[512,1024]{1,0:T(8,128)(2,1)} %bitcast.37), custom_call_target="tpu_custom_call" | custom-call | flops 939524096 | bytes 4000000 | tf_op jit(solution)/shard_map/grad_down_tile/pallas_call | solution.py:56
  148.5 1.5 combine.1
  150.0 5.4 %collective-permute-done.13.g1 = bf16[2,64,1024]{2,1,0:T(8,128)(2,1)} collective-permute-done((bf16[2,64,1024]{2,1,0:T(8,128)(2,1)S(1)}, bf16[2,64,1024]{2,1,0:T(8,128)(2,1)}, u32[]{:S(2)}, u32[]{:S(2)}) %collective-permute-start.13) | collective-permute-done | bytes 262176 | tf_op jit(solution)/shard_map/ppermute | solution.py:239
  155.4 4.3 %grad_tile.1 = (bf16[896,1024]{1,0:T(8,128)(2,1)}, bf16[896,1024]{1,0:T(8,128)(2,1)}) custom-call(bf16[896,512]{1,0:T(8,128)(2,1)S(1)} %turn.1.x_ref, bf16[2,64,1024]{2,1,0:T(8,128)(2,1)S(1)} %pad_maximum_fusion.1.g0, bf16[2,64,1024]{2,1,0:T(8,128)(2,1)} %collective-permute-done.13.g1, bf16[2,64,1024]{2,1,0:T(8,128)(2,1)} %collective-permute-done.14.g2, ...), custom_call_target="tpu_custom_call" | custom-call | flops 1879048192 | bytes 6000000 | tf_op jit(solution)/shard_map/grad_tile/pallas_call | solution.py:56
  (61 shorter events, 24.1 us)
Async XLA Ops:
  3.3 37.6 %all-to-all-start = ((bf16[32,16,896]{2,1,0:T(8,128)(2,1)}), bf16[32,16,896]{2,1,0:T(8,128)(2,1)S(1)}, u32[]{:S(2)}, u32[]{:S(2)}) async-start(bf16[32,16,896]{2,1,0:T(8,128)(2,1)} %bitcast.38), calls=%async_computation | async-start | bytes 1835008 | tf_op jit(solution)/shard_map/all_to_all | solution.py:244
  40.9 42.5 %all-to-all-start.1 = ((bf16[32,16,1024]{2,1,0:T(8,128)(2,1)}), bf16[32,16,1024]{2,1,0:T(8,128)(2,1)S(1)}, u32[]{:S(2)}, u32[]{:S(2)}) async-start(bf16[32,16,1024]{2,1,0:T(8,128)(2,1)} %bitcast.43), calls=%async_computation.1 | async-start | bytes 2097152 | tf_op jit(solution)/shard_map/all_to_all | solution.py:244
  52.4 10.5 %collective-permute-start.4 = (bf16[2,64,1280]{2,1,0:T(8,128)(2,1)}, bf16[2,64,1280]{2,1,0:T(8,128)(2,1)S(1)}, u32[]{:S(2)}, u32[]{:S(2)}) collective-permute-start(bf16[2,64,1280]{2,1,0:T(8,128)(2,1)} %get-tuple-element.51), channel_id=1, source_target_pairs={{0,1},{1,2},{2,3},{3,0},{4,5},{5,6},{6,7},{7,4},{8,9},{9,10},{10,1... | collective-permute-start | bytes 983048 | tf_op jit(solution)/shard_map/ppermute | solution.py:239
  53.7 17.3 %collective-permute-start.5 = (bf16[2,64,1280]{2,1,0:T(8,128)(2,1)}, bf16[2,64,1280]{2,1,0:T(8,128)(2,1)S(1)}, u32[]{:S(2)}, u32[]{:S(2)}) collective-permute-start(bf16[2,64,1280]{2,1,0:T(8,128)(2,1)} %get-tuple-element.52), channel_id=1, source_target_pairs={{0,2},{1,3},{2,0},{3,1},{4,6},{5,7},{6,4},{7,5},{8,10},{9,11},{10,... | collective-permute-start | bytes 983048 | tf_op jit(solution)/shard_map/ppermute | solution.py:239
  56.3 17.3 %collective-permute-start = (bf16[4,64,768]{2,1,0:T(8,128)(2,1)}, bf16[4,64,768]{2,1,0:T(8,128)(2,1)S(1)}, u32[]{:S(2)}, u32[]{:S(2)}) collective-permute-start(bf16[4,64,768]{2,1,0:T(8,128)(2,1)} %get-tuple-element.46), channel_id=1, source_target_pairs={{0,4},{1,5},{2,6},{3,7},{4,0},{5,1},{6,2},{7,3},{8,12},{9,13},{10,... | collective-permute-start | bytes 1179656 | tf_op jit(solution)/shard_map/ppermute | solution.py:239
  56.6 14.4 %collective-permute-start.6 = (bf16[2,64,1280]{2,1,0:T(8,128)(2,1)}, bf16[2,64,1280]{2,1,0:T(8,128)(2,1)S(1)}, u32[]{:S(2)}, u32[]{:S(2)}) collective-permute-start(bf16[2,64,1280]{2,1,0:T(8,128)(2,1)} %get-tuple-element.53), channel_id=1, source_target_pairs={{0,3},{1,0},{2,1},{3,2},{4,7},{5,4},{6,5},{7,6},{8,11},{9,8},{10,9... | collective-permute-start | bytes 983048 | tf_op jit(solution)/shard_map/ppermute | solution.py:239
  72.1 6.4 %collective-permute-start.7 = (bf16[64,1280]{1,0:T(8,128)(2,1)S(1)}, bf16[64,1280]{1,0:T(8,128)(2,1)S(1)}, u32[]{:S(2)}, u32[]{:S(2)}) collective-permute-start(bf16[64,1280]{1,0:T(8,128)(2,1)S(1)} %meet_far.2), channel_id=1, source_target_pairs={{0,4},{1,5},{2,6},{3,7},{4,0},{5,1},{6,2},{7,3},{8,12},{9,13},{10,... | collective-permute-start | bytes 491528 | tf_op jit(solution)/shard_map/ppermute | solution.py:239
  74.7 4.8 %collective-permute-start.1 = (bf16[64,768]{1,0:T(8,128)(2,1)S(1)}, bf16[64,768]{1,0:T(8,128)(2,1)S(1)}, u32[]{:S(2)}, u32[]{:S(2)}) collective-permute-start(bf16[64,768]{1,0:T(8,128)(2,1)S(1)} %get-tuple-element.47), channel_id=1, source_target_pairs={{0,1},{1,2},{2,3},{3,0},{4,5},{5,6},{6,7},{7,4},{8,9},{9,10},{10,1... | collective-permute-start | bytes 294920 | tf_op jit(solution)/shard_map/ppermute | solution.py:239
  76.0 6.2 %collective-permute-start.2 = (bf16[64,768]{1,0:T(8,128)(2,1)S(1)}, bf16[64,768]{1,0:T(8,128)(2,1)S(1)}, u32[]{:S(2)}, u32[]{:S(2)}) collective-permute-start(bf16[64,768]{1,0:T(8,128)(2,1)S(1)} %get-tuple-element.48), channel_id=1, source_target_pairs={{0,2},{1,3},{2,0},{3,1},{4,6},{5,7},{6,4},{7,5},{8,10},{9,11},{10,... | collective-permute-start | bytes 294920 | tf_op jit(solution)/shard_map/ppermute | solution.py:239
  77.4 4.8 %collective-permute-start.3 = (bf16[64,768]{1,0:T(8,128)(2,1)S(1)}, bf16[64,768]{1,0:T(8,128)(2,1)S(1)}, u32[]{:S(2)}, u32[]{:S(2)}) collective-permute-start(bf16[64,768]{1,0:T(8,128)(2,1)S(1)} %get-tuple-element.49), channel_id=1, source_target_pairs={{0,3},{1,0},{2,1},{3,2},{4,7},{5,4},{6,5},{7,6},{8,11},{9,8},{10,9... | collective-permute-start | bytes 294920 | tf_op jit(solution)/shard_map/ppermute | solution.py:239
  83.5 15.9 %all-to-all-start.2 = ((bf16[8,64,1024]{2,1,0:T(8,128)(2,1)}), bf16[8,64,1024]{2,1,0:T(8,128)(2,1)}, u32[]{:S(2)}, u32[]{:S(2)}) async-start(bf16[8,64,1024]{2,1,0:T(8,128)(2,1)} %get-tuple-element.63), calls=%async_computation.2 | async-start | bytes 2097152 | tf_op jit(solution)/shard_map/all_to_all | solution.py:331
  91.8 26.6 %collective-permute-start.8 = (bf16[2,64,1024]{2,1,0:T(8,128)(2,1)}, bf16[2,64,1024]{2,1,0:T(8,128)(2,1)S(1)}, u32[]{:S(2)}, u32[]{:S(2)}) collective-permute-start(bf16[2,64,1024]{2,1,0:T(8,128)(2,1)} %get-tuple-element.58), channel_id=1, source_target_pairs={{0,1},{1,2},{2,3},{3,0},{4,5},{5,6},{6,7},{7,4},{8,9},{9,10},{10,1... | collective-permute-start | bytes 786440 | tf_op jit(solution)/shard_map/ppermute | solution.py:239
  93.2 25.3 %collective-permute-start.9 = (bf16[2,64,1024]{2,1,0:T(8,128)(2,1)}, bf16[2,64,1024]{2,1,0:T(8,128)(2,1)S(1)}, u32[]{:S(2)}, u32[]{:S(2)}) collective-permute-start(bf16[2,64,1024]{2,1,0:T(8,128)(2,1)} %get-tuple-element.59), channel_id=1, source_target_pairs={{0,2},{1,3},{2,0},{3,1},{4,6},{5,7},{6,4},{7,5},{8,10},{9,11},{10,... | collective-permute-start | bytes 786440 | tf_op jit(solution)/shard_map/ppermute | solution.py:239
  95.6 22.9 %collective-permute-start.10 = (bf16[2,64,1024]{2,1,0:T(8,128)(2,1)}, bf16[2,64,1024]{2,1,0:T(8,128)(2,1)S(1)}, u32[]{:S(2)}, u32[]{:S(2)}) collective-permute-start(bf16[2,64,1024]{2,1,0:T(8,128)(2,1)} %get-tuple-element.60), channel_id=1, source_target_pairs={{0,3},{1,0},{2,1},{3,2},{4,7},{5,4},{6,5},{7,6},{8,11},{9,8},{10,9... | collective-permute-start | bytes 786440 | tf_op jit(solution)/shard_map/ppermute | solution.py:239
  103.3 45.0 %all-to-all-start.3 = ((bf16[32,16,896]{2,1,0:T(8,128)(2,1)}), bf16[32,16,896]{2,1,0:T(8,128)(2,1)S(1)}, u32[]{:S(2)}, u32[]{:S(2)}) async-start(bf16[32,16,896]{2,1,0:T(8,128)(2,1)} %bitcast.39), calls=%async_computation.3 | async-start | bytes 1835008 | tf_op jit(solution)/shard_map/all_to_all | solution.py:244
  118.5 6.7 %collective-permute-start.11 = (bf16[64,1024]{1,0:T(8,128)(2,1)S(1)}, bf16[64,1024]{1,0:T(8,128)(2,1)S(1)}, u32[]{:S(2)}, u32[]{:S(2)}) collective-permute-start(bf16[64,1024]{1,0:T(8,128)(2,1)S(1)} %meet_far.3), channel_id=1, source_target_pairs={{0,4},{1,5},{2,6},{3,7},{4,0},{5,1},{6,2},{7,3},{8,12},{9,13},{10,... | collective-permute-start | bytes 393224 | tf_op jit(solution)/shard_map/ppermute | solution.py:239
  125.4 9.4 %collective-permute-start.18 = (bf16[64,1024]{1,0:T(8,128)(2,1)S(1)}, bf16[64,1024]{1,0:T(8,128)(2,1)S(1)}, u32[]{:S(2)}, u32[]{:S(2)}) collective-permute-start(bf16[64,1024]{1,0:T(8,128)(2,1)S(1)} %get-tuple-element.62), channel_id=1, source_target_pairs={{0,3},{1,0},{2,1},{3,2},{4,7},{5,4},{6,5},{7,6},{8,11},{9,8},{10,9... | collective-permute-start | bytes 393224 | tf_op jit(solution)/shard_map/ppermute | solution.py:239
  127.6 8.7 %collective-permute-start.17 = (bf16[64,1024]{1,0:T(8,128)(2,1)S(1)}, bf16[64,1024]{1,0:T(8,128)(2,1)S(1)}, u32[]{:S(2)}, u32[]{:S(2)}) collective-permute-start(bf16[64,1024]{1,0:T(8,128)(2,1)S(1)} %get-tuple-element.62), channel_id=1, source_target_pairs={{0,2},{1,3},{2,0},{3,1},{4,6},{5,7},{6,4},{7,5},{8,10},{9,11},{10,... | collective-permute-start | bytes 393224 | tf_op jit(solution)/shard_map/ppermute | solution.py:239
  133.5 5.9 %collective-permute-start.16 = (bf16[64,1024]{1,0:T(8,128)(2,1)S(1)}, bf16[64,1024]{1,0:T(8,128)(2,1)S(1)}, u32[]{:S(2)}, u32[]{:S(2)}) collective-permute-start(bf16[64,1024]{1,0:T(8,128)(2,1)S(1)} %get-tuple-element.62), channel_id=1, source_target_pairs={{0,1},{1,2},{2,3},{3,0},{4,5},{5,6},{6,7},{7,4},{8,9},{9,10},{10,1... | collective-permute-start | bytes 393224 | tf_op jit(solution)/shard_map/ppermute | solution.py:239
  133.5 6.1 %collective-permute-start.12 = (bf16[64,1024]{1,0:T(8,128)(2,1)S(1)}, bf16[64,1024]{1,0:T(8,128)(2,1)S(1)}, u32[]{:S(2)}, u32[]{:S(2)}) collective-permute-start(bf16[64,1024]{1,0:T(8,128)(2,1)S(1)} %get-tuple-element.61), channel_id=1, source_target_pairs={{0,4},{1,5},{2,6},{3,7},{4,0},{5,1},{6,2},{7,3},{8,12},{9,13},{10,... | collective-permute-start | bytes 393224 | tf_op jit(solution)/shard_map/ppermute | solution.py:239
  139.5 15.9 %collective-permute-start.19 = (bf16[4,64,1024]{2,1,0:T(8,128)(2,1)S(1)}, bf16[4,64,1024]{2,1,0:T(8,128)(2,1)}, u32[]{:S(2)}, u32[]{:S(2)}) collective-permute-start(bf16[4,64,1024]{2,1,0:T(8,128)(2,1)S(1)} %pad_maximum_fusion.u0), channel_id=1, source_target_pairs={{0,4},{1,5},{2,6},{3,7},{4,0},{5,1},{6,2},{7,3},{8,12},{9,13},{10,... | collective-permute-start | bytes 1572872 | tf_op jit(solution)/shard_map/ppermute | solution.py:239
  139.7 10.3 %collective-permute-start.15 = (bf16[2,64,1024]{2,1,0:T(8,128)(2,1)S(1)}, bf16[2,64,1024]{2,1,0:T(8,128)(2,1)S(1)}, u32[]{:S(2)}, u32[]{:S(2)}) collective-permute-start(bf16[2,64,1024]{2,1,0:T(8,128)(2,1)S(1)} %pad_maximum_fusion.1.g0), channel_id=1, source_target_pairs={{0,3},{1,0},{2,1},{3,2},{4,7},{5,4},{6,5},{7,6},{8,11},{9,8},{10,9... | collective-permute-start | bytes 786440 | tf_op jit(solution)/shard_map/ppermute | solution.py:239
  141.1 8.9 %collective-permute-start.14 = (bf16[2,64,1024]{2,1,0:T(8,128)(2,1)S(1)}, bf16[2,64,1024]{2,1,0:T(8,128)(2,1)}, u32[]{:S(2)}, u32[]{:S(2)}) collective-permute-start(bf16[2,64,1024]{2,1,0:T(8,128)(2,1)S(1)} %pad_maximum_fusion.1.g0), channel_id=1, source_target_pairs={{0,2},{1,3},{2,0},{3,1},{4,6},{5,7},{6,4},{7,5},{8,10},{9,11},{10,... | collective-permute-start | bytes 786440 | tf_op jit(solution)/shard_map/ppermute | solution.py:239
  142.3 13.1 %collective-permute-start.13 = (bf16[2,64,1024]{2,1,0:T(8,128)(2,1)S(1)}, bf16[2,64,1024]{2,1,0:T(8,128)(2,1)}, u32[]{:S(2)}, u32[]{:S(2)}) collective-permute-start(bf16[2,64,1024]{2,1,0:T(8,128)(2,1)S(1)} %pad_maximum_fusion.1.g0), channel_id=1, source_target_pairs={{0,1},{1,2},{2,3},{3,0},{4,5},{5,6},{6,7},{7,4},{8,9},{9,10},{10,1... | collective-permute-start | bytes 786440 | tf_op jit(solution)/shard_map/ppermute | solution.py:239
  (9 other events, 43.6 us)

commit v4 on v3

--- a/solution.py
+++ b/solution.py
@@ -343,8 +343,8 @@
     (d_far,) = call(meet_far, [(part, BF16)], *got, flops=10**11)
     got_d = move(d_far, N_Y)
     d_gate, d_up = call(back_act, [(part, BF16)] * 2, gate_pre, up_pre, *got, got_d)
+    got_du = [move(d_up, dy) for dy in range(1, N_Y)]
     got_dg = move(d_gate, N_Y)
-    got_du = [move(d_up, dy) for dy in range(1, N_Y)]
     dg_pair = jnp.stack([d_gate, got_dg])
     du_four = jnp.stack([d_up] + got_du)
     dg = [dg_pair] + [move(dg_pair, dy) for dy in range(1, N_Y)]

time: 161 us -> 161 us (level)
  no operation moved by 1% of the time
where the time goes in v4:
time: 161 us; the launch traced here: 160 us
  starting transfers between devices  63.7 us (40%)
  waiting for transfers between devices  59.6 us (37%)
  Pallas kernels  31.3 us (19%)
  local copies, waits for them, and re-layouts  4.15 us (3%)
    ppermute x20, waiting for transfers between devices, move(): return lax.ppermute(array, 'blk', pairs)  35.9 us
    all_to_all x3, starting transfers between devices, to_experts(): lax.all_to_all(rows.reshape(experts, CAP, cols), 'expert', split_axis=0,...  33.8 us
    pallas_call x14, Pallas kernels, call(): pl.pallas_call(kernel, out_shape=outs, compiler_params=pltpu.CompilerPara...  31.3 us
    ppermute x20, starting transfers between devices, move(): return lax.ppermute(array, 'blk', pairs)  25.6 us
    all_to_all x3, waiting for transfers between devices, to_experts(): lax.all_to_all(rows.reshape(experts, CAP, cols), 'expert', split_axis=0,...  21.1 us
    all_to_all x1, starting transfers between devices, body(): lax.all_to_all(hidden, 'blk', split_axis=0, concat_axis=0, tiled=True)  4.24 us
  transfers between devices with their start and end apart: 24, of which 12 were waited for; matrix products, arithmetic and copies ran while one was open for 1% of the time, Pallas kernels for 15%

profile of v4, /device:TPU:1, one launch (start us, length us, event | category | flops | bytes accessed | tf_op | source)
XLA Modules:
  0.0 159.7 jit_solution(3971682234517755042)
XLA Ops:
  0.6 2.7 %route.1 = bf16[512,896]{1,0:T(8,128)(2,1)} custom-call(s32[8,256]{1,0:T(8,128)} %bitcast.48, bf16[256,896]{1,0:T(8,128)(2,1)} %tok_ref.1), custom_call_target="tpu_custom_call" | custom-call | tf_op jit(solution)/shard_map/route/pallas_call | solution.py:56
  3.3 12.6 %all-to-all-start = ((bf16[32,16,896]{2,1,0:T(8,128)(2,1)}), bf16[32,16,896]{2,1,0:T(8,128)(2,1)S(1)}, u32[]{:S(2)}, u32[]{:S(2)}) async-start(bf16[32,16,896]{2,1,0:T(8,128)(2,1)} %bitcast.38), calls=%async_computation | async-start | bytes 1835008 | tf_op jit(solution)/shard_map/all_to_all | solution.py:244
  16.7 3.2 %route_back.1 = (bf16[512,1024]{1,0:T(8,128)(2,1)}, bf16[256,512]{1,0:T(8,128)(2,1)}, bf16[256,512]{1,0:T(8,128)(2,1)}) custom-call(s32[8,256]{1,0:T(8,128)} %bitcast.49, s32[8,256]{1,0:T(8,128)} %bitcast.50, bf16[256,896]{1,0:T(8,128)(2,1)} %cot_ref.1), custom_call_target="tpu_custom_call" | custom-call | tf_op jit(solution)/shard_map/route_back/pallas_call | solution.py:56
  19.9 21.0 %all-to-all-done = bf16[32,16,896]{2,1,0:T(8,128)(2,1)S(1)} async-done(((bf16[32,16,896]{2,1,0:T(8,128)(2,1)}), bf16[32,16,896]{2,1,0:T(8,128)(2,1)S(1)}, u32[]{:S(2)}, u32[]{:S(2)}) %all-to-all-start) | async-done | bytes 917536 | tf_op jit(solution)/shard_map/all_to_all | solution.py:244
  40.9 6.2 %all-to-all-start.1 = ((bf16[32,16,1024]{2,1,0:T(8,128)(2,1)}), bf16[32,16,1024]{2,1,0:T(8,128)(2,1)S(1)}, u32[]{:S(2)}, u32[]{:S(2)}) async-start(bf16[32,16,1024]{2,1,0:T(8,128)(2,1)} %bitcast.43), calls=%async_computation.1 | async-start | bytes 2097152 | tf_op jit(solution)/shard_map/all_to_all | solution.py:244
  47.1 5.2 %project.1 = (bf16[4,64,768]{2,1,0:T(8,128)(2,1)}, bf16[4,64,768]{2,1,0:T(8,128)(2,1)}, bf16[2,64,1280]{2,1,0:T(8,128)(2,1)}, bf16[2,64,1280]{2,1,0:T(8,128)(2,1...) custom-call(s32[8]{0:T(128)} %stack.70.order_ref, bf16[512,896]{1,0:T(8,128)(2,1)} %bitcast.31, ...), custom_call_target="tpu_custom_call" | custom-call | flops 1879048192 | bytes 7000000 | tf_op jit(solution)/shard_map/project/pallas_call | solution.py:56
  53.7 2.6 %collective-permute-start.5 = (bf16[2,64,1280]{2,1,0:T(8,128)(2,1)}, bf16[2,64,1280]{2,1,0:T(8,128)(2,1)S(1)}, u32[]{:S(2)}, u32[]{:S(2)}) collective-permute-start(bf16[2,64,1280]{2,1,0:T(8,128)(2,1)} %get-tuple-element.52), channel_id=1, source_target_pairs={{0,2},{1,3},{2,0},{3,1},{4,6},{5,7},{6,4},{7,5},{8,10},{9,11},{10,... | collective-permute-start | bytes 983048 | tf_op jit(solution)/shard_map/ppermute | solution.py:239
  57.7 5.2 %collective-permute-done.4.refs_1_.w1 = bf16[2,64,1280]{2,1,0:T(8,128)(2,1)S(1)} collective-permute-done((bf16[2,64,1280]{2,1,0:T(8,128)(2,1)}, bf16[2,64,1280]{2,1,0:T(8,128)(2,1)S(1)}, u32[]{:S(2)}, u32[]{:S(2)}) %collective-permute-start.4) | collective-permute-done | bytes 327712 | tf_op jit(solution)/shard_map/ppermute | solution.py:239
  62.9 8.1 %collective-permute-done.5.refs_2_.w2 = bf16[2,64,1280]{2,1,0:T(8,128)(2,1)S(1)} collective-permute-done((bf16[2,64,1280]{2,1,0:T(8,128)(2,1)}, bf16[2,64,1280]{2,1,0:T(8,128)(2,1)S(1)}, u32[]{:S(2)}, u32[]{:S(2)}) %collective-permute-start.5) | collective-permute-done | bytes 327712 | tf_op jit(solution)/shard_map/ppermute | solution.py:239
  79.4 2.8 %collective-permute-done.2.n2 = bf16[64,768]{1,0:T(8,128)(2,1)S(1)} collective-permute-done((bf16[64,768]{1,0:T(8,128)(2,1)S(1)}, bf16[64,768]{1,0:T(8,128)(2,1)S(1)}, u32[]{:S(2)}, u32[]{:S(2)}) %collective-permute-start.2) | collective-permute-done | bytes 98336 | tf_op jit(solution)/shard_map/ppermute | solution.py:239
  83.5 4.2 %all-to-all-start.2 = ((bf16[8,64,1024]{2,1,0:T(8,128)(2,1)}), bf16[8,64,1024]{2,1,0:T(8,128)(2,1)}, u32[]{:S(2)}, u32[]{:S(2)}) async-start(bf16[8,64,1024]{2,1,0:T(8,128)(2,1)} %get-tuple-element.63), calls=%async_computation.2 | async-start | bytes 2097152 | tf_op jit(solution)/shard_map/all_to_all | solution.py:331
  87.7 4.0 %back.1 = (bf16[2,64,1024]{2,1,0:T(8,128)(2,1)}, bf16[2,64,1024]{2,1,0:T(8,128)(2,1)}, bf16[2,64,1024]{2,1,0:T(8,128)(2,1)}, bf16[2,64,1024]{2,1,0:T(8,128)(2,1)}, s32[8,128]{1,0:T(8,128)}) custom-call(s32[8]{0:T(128)} %stack.70.order_ref, bf16[512,1024]{1,0:T(8,128)(2,1)} %bitcast.36, bf16[1024,896]{1,0:T(8,128)(2,1)} %bitcast.40), custom_call_target="tpu_custom_call" | custom-call | flops 939524096 | bytes 4000000 | tf_op jit(solution)/shard_map/back/pallas_call | solution.py:56
  93.2 2.4 %collective-permute-start.9 = (bf16[2,64,1024]{2,1,0:T(8,128)(2,1)}, bf16[2,64,1024]{2,1,0:T(8,128)(2,1)S(1)}, u32[]{:S(2)}, u32[]{:S(2)}) collective-permute-start(bf16[2,64,1024]{2,1,0:T(8,128)(2,1)} %get-tuple-element.59), channel_id=1, source_target_pairs={{0,2},{1,3},{2,0},{3,1},{4,6},{5,7},{6,4},{7,5},{8,10},{9,11},{10,... | collective-permute-start | bytes 786440 | tf_op jit(solution)/shard_map/ppermute | solution.py:239
  96.7 2.6 %all-to-all-done.2 = bf16[8,64,1024]{2,1,0:T(8,128)(2,1)} async-done(((bf16[8,64,1024]{2,1,0:T(8,128)(2,1)}), bf16[8,64,1024]{2,1,0:T(8,128)(2,1)}, u32[]{:S(2)}, u32[]{:S(2)}) %all-to-all-start.2) | async-done | bytes 1048608 | tf_op jit(solution)/shard_map/all_to_all | solution.py:331
  99.4 4.0 %expert.1 = bf16[512,896]{1,0:T(8,128)(2,1)} custom-call(bf16[1024,896]{1,0:T(8,128)(2,1)} %bitcast.41, bf16[512,1024]{1,0:T(8,128)(2,1)} %bitcast.23.hidden_ref), custom_call_target="tpu_custom_call" | custom-call | flops 939524096 | bytes 4000000 | tf_op jit(solution)/shard_map/expert/pallas_call | solution.py:56
  103.3 15.1 %all-to-all-start.3 = ((bf16[32,16,896]{2,1,0:T(8,128)(2,1)}), bf16[32,16,896]{2,1,0:T(8,128)(2,1)S(1)}, u32[]{:S(2)}, u32[]{:S(2)}) async-start(bf16[32,16,896]{2,1,0:T(8,128)(2,1)} %bitcast.39), calls=%async_computation.3 | async-start | bytes 1835008 | tf_op jit(solution)/shard_map/all_to_all | solution.py:244
  118.8 6.4 %collective-permute-done.11.got = bf16[64,1024]{1,0:T(8,128)(2,1)S(1)} collective-permute-done((bf16[64,1024]{1,0:T(8,128)(2,1)S(1)}, bf16[64,1024]{1,0:T(8,128)(2,1)S(1)}, u32[]{:S(2)}, u32[]{:S(2)}) %collective-permute-start.11) | collective-permute-done | bytes 131104 | tf_op jit(solution)/shard_map/ppermute | solution.py:239
  125.4 2.2 %collective-permute-start.18 = (bf16[64,1024]{1,0:T(8,128)(2,1)S(1)}, bf16[64,1024]{1,0:T(8,128)(2,1)S(1)}, u32[]{:S(2)}, u32[]{:S(2)}) collective-permute-start(bf16[64,1024]{1,0:T(8,128)(2,1)S(1)} %get-tuple-element.62), channel_id=1, source_target_pairs={{0,3},{1,0},{2,1},{3,2},{4,7},{5,4},{6,5},{7,6},{8,11},{9,8},{10,9... | collective-permute-start | bytes 393224 | tf_op jit(solution)/shard_map/ppermute | solution.py:239
  127.6 6.0 %collective-permute-start.17 = (bf16[64,1024]{1,0:T(8,128)(2,1)S(1)}, bf16[64,1024]{1,0:T(8,128)(2,1)S(1)}, u32[]{:S(2)}, u32[]{:S(2)}) collective-permute-start(bf16[64,1024]{1,0:T(8,128)(2,1)S(1)} %get-tuple-element.62), channel_id=1, source_target_pairs={{0,2},{1,3},{2,0},{3,1},{4,6},{5,7},{6,4},{7,5},{8,10},{9,11},{10,... | collective-permute-start | bytes 393224 | tf_op jit(solution)/shard_map/ppermute | solution.py:239
  136.3 3.2 %collective-permute-done.16 = bf16[64,1024]{1,0:T(8,128)(2,1)S(1)} collective-permute-done((bf16[64,1024]{1,0:T(8,128)(2,1)S(1)}, bf16[64,1024]{1,0:T(8,128)(2,1)S(1)}, u32[]{:S(2)}, u32[]{:S(2)}) %collective-permute-start.16) | collective-permute-done | bytes 131104 | tf_op jit(solution)/shard_map/ppermute | solution.py:239
  143.6 3.9 %grad_down_tile.1 = bf16[1024,896]{1,0:T(8,128)(2,1)} custom-call(bf16[512,1024]{1,0:T(8,128)(2,1)} %bitcast.23.hidden_ref, bf16[512,1024]{1,0:T(8,128)(2,1)} %bitcast.37), custom_call_target="tpu_custom_call" | custom-call | flops 939524096 | bytes 4000000 | tf_op jit(solution)/shard_map/grad_down_tile/pallas_call | solution.py:56
  148.5 1.5 combine.1
  150.0 5.4 %collective-permute-done.13.g1 = bf16[2,64,1024]{2,1,0:T(8,128)(2,1)} collective-permute-done((bf16[2,64,1024]{2,1,0:T(8,128)(2,1)S(1)}, bf16[2,64,1024]{2,1,0:T(8,128)(2,1)}, u32[]{:S(2)}, u32[]{:S(2)}) %collective-permute-start.13) | collective-permute-done | bytes 262176 | tf_op jit(solution)/shard_map/ppermute | solution.py:239
  155.4 4.3 %grad_tile.1 = (bf16[896,1024]{1,0:T(8,128)(2,1)}, bf16[896,1024]{1,0:T(8,128)(2,1)}) custom-call(bf16[896,512]{1,0:T(8,128)(2,1)S(1)} %turn.1.x_ref, bf16[2,64,1024]{2,1,0:T(8,128)(2,1)S(1)} %pad_maximum_fusion.1.g0, bf16[2,64,1024]{2,1,0:T(8,128)(2,1)} %collective-permute-done.13.g1, bf16[2,64,1024]{2,1,0:T(8,128)(2,1)} %collective-permute-done.14.g2, ...), custom_call_target="tpu_custom_call" | custom-call | flops 1879048192 | bytes 6000000 | tf_op jit(solution)/shard_map/grad_tile/pallas_call | solution.py:56
  (61 shorter events, 24.1 us)
Async XLA Ops:
  3.3 37.6 %all-to-all-start = ((bf16[32,16,896]{2,1,0:T(8,128)(2,1)}), bf16[32,16,896]{2,1,0:T(8,128)(2,1)S(1)}, u32[]{:S(2)}, u32[]{:S(2)}) async-start(bf16[32,16,896]{2,1,0:T(8,128)(2,1)} %bitcast.38), calls=%async_computation | async-start | bytes 1835008 | tf_op jit(solution)/shard_map/all_to_all | solution.py:244
  40.9 42.5 %all-to-all-start.1 = ((bf16[32,16,1024]{2,1,0:T(8,128)(2,1)}), bf16[32,16,1024]{2,1,0:T(8,128)(2,1)S(1)}, u32[]{:S(2)}, u32[]{:S(2)}) async-start(bf16[32,16,1024]{2,1,0:T(8,128)(2,1)} %bitcast.43), calls=%async_computation.1 | async-start | bytes 2097152 | tf_op jit(solution)/shard_map/all_to_all | solution.py:244
  52.4 10.5 %collective-permute-start.4 = (bf16[2,64,1280]{2,1,0:T(8,128)(2,1)}, bf16[2,64,1280]{2,1,0:T(8,128)(2,1)S(1)}, u32[]{:S(2)}, u32[]{:S(2)}) collective-permute-start(bf16[2,64,1280]{2,1,0:T(8,128)(2,1)} %get-tuple-element.51), channel_id=1, source_target_pairs={{0,1},{1,2},{2,3},{3,0},{4,5},{5,6},{6,7},{7,4},{8,9},{9,10},{10,1... | collective-permute-start | bytes 983048 | tf_op jit(solution)/shard_map/ppermute | solution.py:239
  53.7 17.3 %collective-permute-start.5 = (bf16[2,64,1280]{2,1,0:T(8,128)(2,1)}, bf16[2,64,1280]{2,1,0:T(8,128)(2,1)S(1)}, u32[]{:S(2)}, u32[]{:S(2)}) collective-permute-start(bf16[2,64,1280]{2,1,0:T(8,128)(2,1)} %get-tuple-element.52), channel_id=1, source_target_pairs={{0,2},{1,3},{2,0},{3,1},{4,6},{5,7},{6,4},{7,5},{8,10},{9,11},{10,... | collective-permute-start | bytes 983048 | tf_op jit(solution)/shard_map/ppermute | solution.py:239
  56.3 17.3 %collective-permute-start = (bf16[4,64,768]{2,1,0:T(8,128)(2,1)}, bf16[4,64,768]{2,1,0:T(8,128)(2,1)S(1)}, u32[]{:S(2)}, u32[]{:S(2)}) collective-permute-start(bf16[4,64,768]{2,1,0:T(8,128)(2,1)} %get-tuple-element.46), channel_id=1, source_target_pairs={{0,4},{1,5},{2,6},{3,7},{4,0},{5,1},{6,2},{7,3},{8,12},{9,13},{10,... | collective-permute-start | bytes 1179656 | tf_op jit(solution)/shard_map/ppermute | solution.py:239
  56.6 14.4 %collective-permute-start.6 = (bf16[2,64,1280]{2,1,0:T(8,128)(2,1)}, bf16[2,64,1280]{2,1,0:T(8,128)(2,1)S(1)}, u32[]{:S(2)}, u32[]{:S(2)}) collective-permute-start(bf16[2,64,1280]{2,1,0:T(8,128)(2,1)} %get-tuple-element.53), channel_id=1, source_target_pairs={{0,3},{1,0},{2,1},{3,2},{4,7},{5,4},{6,5},{7,6},{8,11},{9,8},{10,9... | collective-permute-start | bytes 983048 | tf_op jit(solution)/shard_map/ppermute | solution.py:239
  72.1 6.4 %collective-permute-start.7 = (bf16[64,1280]{1,0:T(8,128)(2,1)S(1)}, bf16[64,1280]{1,0:T(8,128)(2,1)S(1)}, u32[]{:S(2)}, u32[]{:S(2)}) collective-permute-start(bf16[64,1280]{1,0:T(8,128)(2,1)S(1)} %meet_far.2), channel_id=1, source_target_pairs={{0,4},{1,5},{2,6},{3,7},{4,0},{5,1},{6,2},{7,3},{8,12},{9,13},{10,... | collective-permute-start | bytes 491528 | tf_op jit(solution)/shard_map/ppermute | solution.py:239
  74.7 4.8 %collective-permute-start.1 = (bf16[64,768]{1,0:T(8,128)(2,1)S(1)}, bf16[64,768]{1,0:T(8,128)(2,1)S(1)}, u32[]{:S(2)}, u32[]{:S(2)}) collective-permute-start(bf16[64,768]{1,0:T(8,128)(2,1)S(1)} %get-tuple-element.47), channel_id=1, source_target_pairs={{0,1},{1,2},{2,3},{3,0},{4,5},{5,6},{6,7},{7,4},{8,9},{9,10},{10,1... | collective-permute-start | bytes 294920 | tf_op jit(solution)/shard_map/ppermute | solution.py:239
  76.0 6.2 %collective-permute-start.2 = (bf16[64,768]{1,0:T(8,128)(2,1)S(1)}, bf16[64,768]{1,0:T(8,128)(2,1)S(1)}, u32[]{:S(2)}, u32[]{:S(2)}) collective-permute-start(bf16[64,768]{1,0:T(8,128)(2,1)S(1)} %get-tuple-element.48), channel_id=1, source_target_pairs={{0,2},{1,3},{2,0},{3,1},{4,6},{5,7},{6,4},{7,5},{8,10},{9,11},{10,... | collective-permute-start | bytes 294920 | tf_op jit(solution)/shard_map/ppermute | solution.py:239
  77.4 4.8 %collective-permute-start.3 = (bf16[64,768]{1,0:T(8,128)(2,1)S(1)}, bf16[64,768]{1,0:T(8,128)(2,1)S(1)}, u32[]{:S(2)}, u32[]{:S(2)}) collective-permute-start(bf16[64,768]{1,0:T(8,128)(2,1)S(1)} %get-tuple-element.49), channel_id=1, source_target_pairs={{0,3},{1,0},{2,1},{3,2},{4,7},{5,4},{6,5},{7,6},{8,11},{9,8},{10,9... | collective-permute-start | bytes 294920 | tf_op jit(solution)/shard_map/ppermute | solution.py:239
  83.5 15.9 %all-to-all-start.2 = ((bf16[8,64,1024]{2,1,0:T(8,128)(2,1)}), bf16[8,64,1024]{2,1,0:T(8,128)(2,1)}, u32[]{:S(2)}, u32[]{:S(2)}) async-start(bf16[8,64,1024]{2,1,0:T(8,128)(2,1)} %get-tuple-element.63), calls=%async_computation.2 | async-start | bytes 2097152 | tf_op jit(solution)/shard_map/all_to_all | solution.py:331
  91.8 26.6 %collective-permute-start.8 = (bf16[2,64,1024]{2,1,0:T(8,128)(2,1)}, bf16[2,64,1024]{2,1,0:T(8,128)(2,1)S(1)}, u32[]{:S(2)}, u32[]{:S(2)}) collective-permute-start(bf16[2,64,1024]{2,1,0:T(8,128)(2,1)} %get-tuple-element.58), channel_id=1, source_target_pairs={{0,1},{1,2},{2,3},{3,0},{4,5},{5,6},{6,7},{7,4},{8,9},{9,10},{10,1... | collective-permute-start | bytes 786440 | tf_op jit(solution)/shard_map/ppermute | solution.py:239
  93.2 25.3 %collective-permute-start.9 = (bf16[2,64,1024]{2,1,0:T(8,128)(2,1)}, bf16[2,64,1024]{2,1,0:T(8,128)(2,1)S(1)}, u32[]{:S(2)}, u32[]{:S(2)}) collective-permute-start(bf16[2,64,1024]{2,1,0:T(8,128)(2,1)} %get-tuple-element.59), channel_id=1, source_target_pairs={{0,2},{1,3},{2,0},{3,1},{4,6},{5,7},{6,4},{7,5},{8,10},{9,11},{10,... | collective-permute-start | bytes 786440 | tf_op jit(solution)/shard_map/ppermute | solution.py:239
  95.6 22.9 %collective-permute-start.10 = (bf16[2,64,1024]{2,1,0:T(8,128)(2,1)}, bf16[2,64,1024]{2,1,0:T(8,128)(2,1)S(1)}, u32[]{:S(2)}, u32[]{:S(2)}) collective-permute-start(bf16[2,64,1024]{2,1,0:T(8,128)(2,1)} %get-tuple-element.60), channel_id=1, source_target_pairs={{0,3},{1,0},{2,1},{3,2},{4,7},{5,4},{6,5},{7,6},{8,11},{9,8},{10,9... | collective-permute-start | bytes 786440 | tf_op jit(solution)/shard_map/ppermute | solution.py:239
  103.3 45.0 %all-to-all-start.3 = ((bf16[32,16,896]{2,1,0:T(8,128)(2,1)}), bf16[32,16,896]{2,1,0:T(8,128)(2,1)S(1)}, u32[]{:S(2)}, u32[]{:S(2)}) async-start(bf16[32,16,896]{2,1,0:T(8,128)(2,1)} %bitcast.39), calls=%async_computation.3 | async-start | bytes 1835008 | tf_op jit(solution)/shard_map/all_to_all | solution.py:244
  118.5 6.7 %collective-permute-start.11 = (bf16[64,1024]{1,0:T(8,128)(2,1)S(1)}, bf16[64,1024]{1,0:T(8,128)(2,1)S(1)}, u32[]{:S(2)}, u32[]{:S(2)}) collective-permute-start(bf16[64,1024]{1,0:T(8,128)(2,1)S(1)} %meet_far.3), channel_id=1, source_target_pairs={{0,4},{1,5},{2,6},{3,7},{4,0},{5,1},{6,2},{7,3},{8,12},{9,13},{10,... | collective-permute-start | bytes 393224 | tf_op jit(solution)/shard_map/ppermute | solution.py:239
  125.4 9.4 %collective-permute-start.18 = (bf16[64,1024]{1,0:T(8,128)(2,1)S(1)}, bf16[64,1024]{1,0:T(8,128)(2,1)S(1)}, u32[]{:S(2)}, u32[]{:S(2)}) collective-permute-start(bf16[64,1024]{1,0:T(8,128)(2,1)S(1)} %get-tuple-element.62), channel_id=1, source_target_pairs={{0,3},{1,0},{2,1},{3,2},{4,7},{5,4},{6,5},{7,6},{8,11},{9,8},{10,9... | collective-permute-start | bytes 393224 | tf_op jit(solution)/shard_map/ppermute | solution.py:239
  127.6 8.7 %collective-permute-start.17 = (bf16[64,1024]{1,0:T(8,128)(2,1)S(1)}, bf16[64,1024]{1,0:T(8,128)(2,1)S(1)}, u32[]{:S(2)}, u32[]{:S(2)}) collective-permute-start(bf16[64,1024]{1,0:T(8,128)(2,1)S(1)} %get-tuple-element.62), channel_id=1, source_target_pairs={{0,2},{1,3},{2,0},{3,1},{4,6},{5,7},{6,4},{7,5},{8,10},{9,11},{10,... | collective-permute-start | bytes 393224 | tf_op jit(solution)/shard_map/ppermute | solution.py:239
  133.5 5.9 %collective-permute-start.16 = (bf16[64,1024]{1,0:T(8,128)(2,1)S(1)}, bf16[64,1024]{1,0:T(8,128)(2,1)S(1)}, u32[]{:S(2)}, u32[]{:S(2)}) collective-permute-start(bf16[64,1024]{1,0:T(8,128)(2,1)S(1)} %get-tuple-element.62), channel_id=1, source_target_pairs={{0,1},{1,2},{2,3},{3,0},{4,5},{5,6},{6,7},{7,4},{8,9},{9,10},{10,1... | collective-permute-start | bytes 393224 | tf_op jit(solution)/shard_map/ppermute | solution.py:239
  133.5 6.1 %collective-permute-start.12 = (bf16[64,1024]{1,0:T(8,128)(2,1)S(1)}, bf16[64,1024]{1,0:T(8,128)(2,1)S(1)}, u32[]{:S(2)}, u32[]{:S(2)}) collective-permute-start(bf16[64,1024]{1,0:T(8,128)(2,1)S(1)} %get-tuple-element.61), channel_id=1, source_target_pairs={{0,4},{1,5},{2,6},{3,7},{4,0},{5,1},{6,2},{7,3},{8,12},{9,13},{10,... | collective-permute-start | bytes 393224 | tf_op jit(solution)/shard_map/ppermute | solution.py:239
  139.5 15.9 %collective-permute-start.19 = (bf16[4,64,1024]{2,1,0:T(8,128)(2,1)S(1)}, bf16[4,64,1024]{2,1,0:T(8,128)(2,1)}, u32[]{:S(2)}, u32[]{:S(2)}) collective-permute-start(bf16[4,64,1024]{2,1,0:T(8,128)(2,1)S(1)} %pad_maximum_fusion.u0), channel_id=1, source_target_pairs={{0,4},{1,5},{2,6},{3,7},{4,0},{5,1},{6,2},{7,3},{8,12},{9,13},{10,... | collective-permute-start | bytes 1572872 | tf_op jit(solution)/shard_map/ppermute | solution.py:239
  139.7 10.3 %collective-permute-start.15 = (bf16[2,64,1024]{2,1,0:T(8,128)(2,1)S(1)}, bf16[2,64,1024]{2,1,0:T(8,128)(2,1)S(1)}, u32[]{:S(2)}, u32[]{:S(2)}) collective-permute-start(bf16[2,64,1024]{2,1,0:T(8,128)(2,1)S(1)} %pad_maximum_fusion.1.g0), channel_id=1, source_target_pairs={{0,3},{1,0},{2,1},{3,2},{4,7},{5,4},{6,5},{7,6},{8,11},{9,8},{10,9... | collective-permute-start | bytes 786440 | tf_op jit(solution)/shard_map/ppermute | solution.py:239
  141.1 8.9 %collective-permute-start.14 = (bf16[2,64,1024]{2,1,0:T(8,128)(2,1)S(1)}, bf16[2,64,1024]{2,1,0:T(8,128)(2,1)}, u32[]{:S(2)}, u32[]{:S(2)}) collective-permute-start(bf16[2,64,1024]{2,1,0:T(8,128)(2,1)S(1)} %pad_maximum_fusion.1.g0), channel_id=1, source_target_pairs={{0,2},{1,3},{2,0},{3,1},{4,6},{5,7},{6,4},{7,5},{8,10},{9,11},{10,... | collective-permute-start | bytes 786440 | tf_op jit(solution)/shard_map/ppermute | solution.py:239
  142.3 13.1 %collective-permute-start.13 = (bf16[2,64,1024]{2,1,0:T(8,128)(2,1)S(1)}, bf16[2,64,1024]{2,1,0:T(8,128)(2,1)}, u32[]{:S(2)}, u32[]{:S(2)}) collective-permute-start(bf16[2,64,1024]{2,1,0:T(8,128)(2,1)S(1)} %pad_maximum_fusion.1.g0), channel_id=1, source_target_pairs={{0,1},{1,2},{2,3},{3,0},{4,5},{5,6},{6,7},{7,4},{8,9},{9,10},{10,1... | collective-permute-start | bytes 786440 | tf_op jit(solution)/shard_map/ppermute | solution.py:239
  (9 other events, 43.6 us)
